TPU v7x, 32 devices: a whole 2x2x4 slice. The times are simulated.
32 devices in a mesh: ex: 8 (over z, x), tp: 4 (over y, core).
Axes of the slice: x: 2, y: 2, z: 4, core: 2. Of those that a mesh axis runs over, the one named last changes fastest.
Arguments:
- inputs: bfloat16 [1024, 768], P('ex'), may hold values from -6 to 6
- routes: int32 [1024, 2], P('ex'), may hold values from 0 to 7, all different within a row; in each aligned block of 128 rows (0 to 127, 128 to 255, ...) at most 64 rows name the same one
- lengths: int32 [8, 4], P('ex'), may hold values from 1 to 96, 128 in all within a row
- w_query: bfloat16 [768, 768], P(None, 'tp'), may hold values from -0.21875 to 0.21875
- w_key: bfloat16 [768, 768], P(None, 'tp'), may hold values from -0.21875 to 0.21875
- w_value: bfloat16 [768, 768], P(None, 'tp'), may hold values from -0.21875 to 0.21875
- w_attn_out: bfloat16 [768, 768], P('tp'), may hold values from -0.875 to 0.875
- gain_attn: float32 [768], replicated, may hold values from 0.25 to 1.75
- gain_moe: float32 [768], replicated, may hold values from 0.25 to 1.75
- rel_bias: float32 [32, 12], P(None, 'tp'), may hold values from -4 to 4
- w_router: bfloat16 [768, 8], replicated, may hold values from -0.15625 to 0.15625
- w_in: bfloat16 [8, 768, 3072], P('ex', None, 'tp'), may hold values from -0.21875 to 0.21875
- w_out: bfloat16 [8, 3072, 768], P('ex', 'tp'), may hold values from -0.109375 to 0.109375
- cotangent: bfloat16 [1024, 768], P('ex'), may hold values from -6 to 6
Outputs:
- output: bfloat16 [1024, 768], P('ex')
- grad_inputs: bfloat16 [1024, 768], P('ex')
- grad_w_query: float32 [768, 768], P(None, 'tp')
- grad_w_key: float32 [768, 768], P(None, 'tp')
- grad_w_value: float32 [768, 768], P(None, 'tp')
- grad_w_attn_out: float32 [768, 768], P('tp')
- grad_gain_attn: float32 [768], replicated
- grad_gain_moe: float32 [768], replicated
- grad_rel_bias: float32 [32, 12], P(None, 'tp')
- grad_w_router: float32 [768, 8], replicated
- grad_w_in: float32 [8, 768, 3072], P('ex', None, 'tp')
- grad_w_out: float32 [8, 3072, 768], P('ex', 'tp')
Inputs may be any that keep to these rules, and one draw needn't show every extreme that they name: `routes`: each row names two different experts. The rows of one index of ex name any one expert at most 64 times, a bound that some block reaches. `lengths`: each row sums to 128 and its largest entry is exactly 96.
All inputs are finite; a program needn't handle non-finite values.
Results may differ from a plain program's by a relative error of at most 0.017.
Values may be sent and summed in bfloat16 or wider, within the bound.
A program may use at most 128 MiB of HBM per device.

v0:
```python
from functools import partial
import math

import jax
import jax.numpy as jnp
from jax import lax
from jax.sharding import PartitionSpec as P

eps = 1e-06
highest = lax.Precision.HIGHEST
bucket_edges = [math.ceil(16 * 8 ** (number / 16)) for number in range(1, 16)]


def rms_scale(values):
    return lax.rsqrt(jnp.mean(values * values, -1, keepdims=True) + eps)


def bucket_of(length):
    positions = jnp.arange(length, dtype=jnp.int32)
    offsets = positions[:, None] - positions[None, :]
    distance = jnp.maximum(offsets, 0)
    counted = jnp.zeros_like(distance)
    for border in bucket_edges:
        counted = counted + (distance >= border).astype(jnp.int32)
    return jnp.where(distance < 16, distance, 16 + counted)


def contract_rows(left_side, right_side):
    return lax.dot_general(
        left_side, right_side, (((0,), (0,)), ((), ())), preferred_element_type=jnp.float32
    )


def contract_cols(left_side, right_side):
    return lax.dot_general(
        left_side, right_side, (((1,), (1,)), ((), ())), preferred_element_type=jnp.float32
    )


def shards(
    inputs,
    routes,
    lengths,
    w_query,
    w_key,
    w_value,
    w_attn_out,
    gain_attn,
    gain_moe,
    rel_bias,
    w_router,
    w_in,
    w_out,
    cotangent,
):
    tok_rows, model_width = inputs.shape
    local_heads = rel_bias.shape[1]
    head_dim = w_query.shape[1] // local_heads
    attn_scale = head_dim ** (-0.5)
    experts = w_router.shape[1]
    ex_devices = lax.axis_size("ex")
    local_experts = w_in.shape[0]
    capacity = 4 * tok_rows // experts
    pair_count = 2 * tok_rows
    inputs_f = inputs.astype(jnp.float32)
    scale_a = rms_scale(inputs_f)
    normed_a = inputs_f * scale_a
    attn_in = (normed_a * gain_attn).astype(jnp.bfloat16)
    query_b = (
        jnp.dot(attn_in, w_query, preferred_element_type=jnp.float32)
        .astype(jnp.bfloat16)
        .reshape(tok_rows, local_heads, head_dim)
    )
    key_b = (
        jnp.dot(attn_in, w_key, preferred_element_type=jnp.float32)
        .astype(jnp.bfloat16)
        .reshape(tok_rows, local_heads, head_dim)
    )
    value_b = (
        jnp.dot(attn_in, w_value, preferred_element_type=jnp.float32)
        .astype(jnp.bfloat16)
        .reshape(tok_rows, local_heads, head_dim)
    )
    buckets = bucket_of(tok_rows)
    one_hot = (
        buckets[None] == jnp.arange(rel_bias.shape[0], dtype=jnp.int32)[:, None, None]
    ).astype(jnp.float32)
    bias_full = jnp.einsum("bij,bh->hij", one_hot, rel_bias, precision=highest)
    seq_ends = jnp.cumsum(lengths[0])
    positions = jnp.arange(tok_rows, dtype=jnp.int32)
    segments = jnp.sum((positions[:, None] >= seq_ends[None, :]).astype(jnp.int32), -1)
    allowed = (segments[:, None] == segments[None, :]) & (positions[:, None] >= positions[None, :])

    def score_of(queries_in, keys_in):
        raw_scores = (
            jnp.einsum("ihd,jhd->hij", queries_in, keys_in, preferred_element_type=jnp.float32)
            * attn_scale
        )
        return jnp.where(allowed[None], raw_scores + bias_full, -1e30)

    scores = score_of(query_b, key_b)
    row_max = jnp.max(scores, -1, keepdims=True)
    log_sum = row_max + jnp.log(jnp.sum(jnp.exp(scores - row_max), -1, keepdims=True))
    probabilities = jnp.exp(scores - log_sum)
    probs_low = probabilities.astype(jnp.bfloat16)
    mixed_heads = (
        jnp.einsum("hij,jhd->ihd", probs_low, value_b, preferred_element_type=jnp.float32)
        .astype(jnp.bfloat16)
        .reshape(tok_rows, -1)
    )
    head_part = jnp.dot(mixed_heads, w_attn_out, preferred_element_type=jnp.float32)
    residual = inputs_f + lax.psum(head_part, "tp")
    scale_m = rms_scale(residual)
    normed_m = residual * scale_m
    moe_in = (normed_m * gain_moe).astype(jnp.bfloat16)
    logits = jnp.dot(moe_in, w_router, preferred_element_type=jnp.float32)
    expert_ids = jnp.arange(experts, dtype=jnp.int32)
    route_hot = (routes[:, :, None] == expert_ids[None, None, :]).astype(jnp.float32)
    chosen_logits = jnp.sum(route_hot * logits[:, None, :], -1)
    gate_max = jnp.max(chosen_logits, -1, keepdims=True)
    gate_exp = jnp.exp(chosen_logits - gate_max)
    gate_values = gate_exp / jnp.sum(gate_exp, -1, keepdims=True)
    pair_routes = routes.reshape(-1)
    pair_hot = (pair_routes[:, None] == expert_ids[None, :]).astype(jnp.int32)
    slot_index = jnp.sum(pair_hot * jnp.cumsum(pair_hot, 0), -1) - 1
    pair_slots = pair_routes * capacity + slot_index
    members = (
        jnp.full((experts * capacity,), pair_count, jnp.int32)
        .at[pair_slots]
        .set(jnp.arange(pair_count, dtype=jnp.int32))
    )
    padded = jnp.concatenate([moe_in, jnp.zeros((1, model_width), jnp.bfloat16)], 0)
    send_rows = padded[members // 2].reshape(experts, capacity, model_width)
    arrived = lax.all_to_all(send_rows, "ex", split_axis=0, concat_axis=0, tiled=True)
    slot_count = arrived.shape[1]
    grouped = arrived.reshape(ex_devices, local_experts, slot_count, model_width)
    pre_act = jnp.einsum("slcd,ldf->slcf", grouped, w_in, preferred_element_type=jnp.float32)
    act_low = jax.nn.gelu(pre_act, approximate=True).astype(jnp.bfloat16)
    partial_out = jnp.einsum("slcf,lfd->slcd", act_low, w_out, preferred_element_type=jnp.float32)
    partial_out = partial_out.reshape(ex_devices * local_experts, slot_count, model_width)
    owned_rows = lax.psum_scatter(
        partial_out.astype(jnp.bfloat16), "tp", scatter_dimension=2, tiled=True
    )
    returned = lax.all_to_all(owned_rows, "ex", split_axis=0, concat_axis=0, tiled=True)
    returned, kept_rows, kept_pre = (
        returned,
        arrived,
        pre_act.reshape(ex_devices * local_experts, slot_count, -1),
    )
    expert_out = lax.all_gather(returned, "tp", axis=2, tiled=True).reshape(
        experts * capacity, model_width
    )
    pair_out = expert_out[pair_slots].reshape(tok_rows, 2, model_width).astype(jnp.float32)
    result = residual + jnp.sum(gate_values[:, :, None] * pair_out, 1)
    output = result.astype(jnp.bfloat16)
    grad_out = cotangent.astype(jnp.float32)
    gate_grad = jnp.sum(grad_out[:, None, :] * pair_out, -1)
    logit_pair = gate_values * (gate_grad - jnp.sum(gate_values * gate_grad, -1, keepdims=True))
    logit_grads = jnp.sum(logit_pair[:, :, None] * route_hot, 1)
    grad_router = jnp.dot(moe_in.astype(jnp.float32).T, logit_grads, precision=highest)
    moe_grad = jnp.dot(logit_grads, w_router.astype(jnp.float32).T, precision=highest)
    pair_grads = (
        (gate_values[:, :, None] * grad_out[:, None, :])
        .astype(jnp.bfloat16)
        .reshape(pair_count, model_width)
    )
    padded_grads = jnp.concatenate([pair_grads, jnp.zeros((1, model_width), jnp.bfloat16)], 0)
    send_grad_rows = padded_grads[members].reshape(experts, capacity, model_width)
    arrived_grads = lax.all_to_all(send_grad_rows, "ex", split_axis=0, concat_axis=0, tiled=True)
    grad_group = arrived_grads.reshape(ex_devices, local_experts, capacity, model_width)
    act_grad = jnp.einsum("slcd,lfd->slcf", grad_group, w_out, preferred_element_type=jnp.float32)
    pre_keep = kept_pre.reshape(ex_devices, local_experts, capacity, -1)
    act_value, gelu_back = jax.vjp(partial(jax.nn.gelu, approximate=True), pre_keep)
    pre_grad = gelu_back(act_grad)[0].astype(jnp.bfloat16)
    act_low = act_value.astype(jnp.bfloat16)
    grad_w_out = jnp.einsum(
        "slcf,slcd->lfd", act_low, grad_group, preferred_element_type=jnp.float32
    )
    rows_group = kept_rows.reshape(ex_devices, local_experts, capacity, model_width)
    grad_w_in = jnp.einsum(
        "slcd,slcf->ldf", rows_group, pre_grad, preferred_element_type=jnp.float32
    )
    row_part = jnp.einsum("slcf,ldf->slcd", pre_grad, w_in, preferred_element_type=jnp.float32)
    row_part = row_part.reshape(ex_devices * local_experts, capacity, model_width)
    row_share = lax.psum_scatter(row_part, "tp", scatter_dimension=2, tiled=True).astype(
        jnp.bfloat16
    )
    row_back = lax.all_to_all(row_share, "ex", split_axis=0, concat_axis=0, tiled=True)
    row_full = lax.all_gather(row_back, "tp", axis=2, tiled=True).reshape(
        experts * capacity, model_width
    )
    moe_grad = moe_grad + jnp.sum(
        row_full[pair_slots].reshape(tok_rows, 2, model_width).astype(jnp.float32), 1
    )
    grad_gain_moe = jnp.sum(moe_grad * normed_m, 0)
    normed_grad_m = moe_grad * gain_moe
    resid_grad = grad_out + scale_m * (
        normed_grad_m - normed_m * jnp.mean(normed_grad_m * normed_m, -1, keepdims=True)
    )
    attn_grad = resid_grad.astype(jnp.bfloat16)
    grad_w_attn_out = contract_rows(mixed_heads, attn_grad)
    mixed_grad = (
        contract_cols(attn_grad, w_attn_out)
        .astype(jnp.bfloat16)
        .reshape(tok_rows, local_heads, head_dim)
    )
    scores_again = score_of(query_b, key_b)
    probs_again = jnp.exp(scores_again - log_sum)
    prob_grad = jnp.einsum("ihd,jhd->hij", mixed_grad, value_b, preferred_element_type=jnp.float32)
    value_grad = jnp.einsum(
        "hij,ihd->jhd",
        probs_again.astype(jnp.bfloat16),
        mixed_grad,
        preferred_element_type=jnp.float32,
    ).astype(jnp.bfloat16)
    score_grad = probs_again * (prob_grad - jnp.sum(probs_again * prob_grad, -1, keepdims=True))
    grad_rel_bias = jnp.einsum("hij,bij->bh", score_grad, one_hot, precision=highest)
    score_low = score_grad.astype(jnp.bfloat16)
    query_grad = (
        (
            jnp.einsum("hij,jhd->ihd", score_low, key_b, preferred_element_type=jnp.float32)
            * attn_scale
        )
        .astype(jnp.bfloat16)
        .reshape(tok_rows, -1)
    )
    key_grad = (
        (
            jnp.einsum("hij,ihd->jhd", score_low, query_b, preferred_element_type=jnp.float32)
            * attn_scale
        )
        .astype(jnp.bfloat16)
        .reshape(tok_rows, -1)
    )
    value_flat = value_grad.reshape(tok_rows, -1)
    grad_w_query = contract_rows(attn_in, query_grad)
    grad_w_key = contract_rows(attn_in, key_grad)
    grad_w_value = contract_rows(attn_in, value_flat)
    input_part = (
        contract_cols(query_grad, w_query)
        + contract_cols(key_grad, w_key)
        + contract_cols(value_flat, w_value)
    )
    input_grad = lax.psum(input_part.astype(jnp.bfloat16), "tp").astype(jnp.float32)
    grad_gain_attn = jnp.sum(input_grad * normed_a, 0)
    normed_grad_a = input_grad * gain_attn
    grad_inputs = (
        resid_grad
        + scale_a
        * (normed_grad_a - normed_a * jnp.mean(normed_grad_a * normed_a, -1, keepdims=True))
    ).astype(jnp.bfloat16)
    dense_sums = lax.psum(
        (
            grad_w_query,
            grad_w_key,
            grad_w_value,
            grad_w_attn_out,
            grad_gain_attn,
            grad_gain_moe,
            grad_rel_bias,
            grad_router,
        ),
        "ex",
    )
    return (
        output,
        grad_inputs,
        dense_sums[0],
        dense_sums[1],
        dense_sums[2],
        dense_sums[3],
        dense_sums[4],
        dense_sums[5],
        dense_sums[6],
        dense_sums[7],
        grad_w_in,
        grad_w_out,
    )


def solution(mesh):
    placed = (
        P("ex", None),
        P("ex", None),
        P("ex", None),
        P(None, "tp"),
        P(None, "tp"),
        P(None, "tp"),
        P("tp", None),
        P(),
        P(),
        P(None, "tp"),
        P(),
        P("ex", None, "tp"),
        P("ex", "tp", None),
        P("ex", None),
    )
    return jax.shard_map(
        shards,
        mesh=mesh,
        in_specs=placed,
        out_specs=(
            P("ex", None),
            P("ex", None),
            P(None, "tp"),
            P(None, "tp"),
            P(None, "tp"),
            P("tp", None),
            P(),
            P(),
            P(None, "tp"),
            P(),
            P("ex", None, "tp"),
            P("ex", "tp", None),
        ),
        check_vma=False,
    )
```

profile of v0, /device:TPU:0, one launch (start us, length us, event | category | flops | bytes accessed | tf_op | source)
XLA Modules:
  0.0 362.4 jit_solution(3472108545965280200)
XLA Ops:
  7.4 1.2 fusion.41
  8.7 1.4 fusion.1
  10.3 1.4 convolution_convert_fusion.6
  16.6 1.4 scatter_custom_fusion
  18.6 31.8 %all-reduce.8.cloned.1.call-done = f32[128,768]{1,0:T(8,128)} async-done(((f32[128,768]{1,0:T(8,128)}), f32[128,768]{1,0:T(8,128)}) %all-reduce.8.cloned.1.call-update) | async-done | bytes 393232 | tf_op jit(solution)/shard_map/psum | solution.py:112
  50.4 1.1 multiply_reduce_fusion.4
  52.9 2.7 gather_fusion
  55.6 5.6 %all-to-all-start = ((bf16[8,64,768]{2,1,0:T(8,128)(2,1)}), bf16[8,64,768]{2,1,0:T(8,128)(2,1)}, u32[]{:S(2)}, u32[]{:S(2)}) async-start(bf16[8,64,768]{2,1,0:T(8,128)(2,1)} %bitcast.13), calls=%async_computation | async-start | bytes 1572864 | tf_op jit(solution)/shard_map/all_to_all | solution.py:134
  65.4 2.7 gather_fusion.2
  68.1 12.4 %all-to-all-done = bf16[8,64,768]{2,1,0:T(8,128)(2,1)} async-done(((bf16[8,64,768]{2,1,0:T(8,128)(2,1)}), bf16[8,64,768]{2,1,0:T(8,128)(2,1)}, u32[]{:S(2)}, u32[]{:S(2)}) %all-to-all-start) | async-done | bytes 786464 | tf_op jit(solution)/shard_map/all_to_all | solution.py:134
  80.5 4.3 %all-to-all-start.2 = ((bf16[8,64,768]{2,1,0:T(8,128)(2,1)}), bf16[8,64,768]{2,1,0:T(8,128)(2,1)}, u32[]{:S(2)}, u32[]{:S(2)}) async-start(bf16[8,64,768]{2,1,0:T(8,128)(2,1)} %bitcast.25), calls=%async_computation.2 | async-start | bytes 1572864 | tf_op jit(solution)/shard_map/all_to_all | solution.py:169
  84.9 1.9 fusion.18
  86.8 1.1 copy-done.46
  87.9 1.9 convolution_convert_fusion
  89.9 2.0 copy.96
  91.9 1.7 reshape.490
  93.9 10.5 %all-to-all-done.2 = bf16[8,64,768]{2,1,0:T(8,128)(2,1)} async-done(((bf16[8,64,768]{2,1,0:T(8,128)(2,1)}), bf16[8,64,768]{2,1,0:T(8,128)(2,1)}, u32[]{:S(2)}, u32[]{:S(2)}) %all-to-all-start.2) | async-done | bytes 786464 | tf_op jit(solution)/shard_map/all_to_all | solution.py:169
  104.4 3.1 fusion.13
  108.4 2.1 fusion.16
  110.5 2.3 copy.98
  112.7 3.7 %reshape.492 = f32[768,512]{1,0:T(8,128)} reshape(f32[768,8,64]{2,1,0:T(8,128)} %bitcast.149) | data formatting | bytes 3145728
  116.5 1.4 reduce-scatter.7.cloned.1.call-done
  117.9 1.2 reshape.491
  120.1 5.5 %all-to-all-start.1 = ((bf16[8,64,192]{2,1,0:T(8,128)(2,1)}), bf16[8,64,192]{2,1,0:T(8,128)(2,1)S(1)}, u32[]{:S(2)}, u32[]{:S(2)}) async-start(bf16[8,64,192]{2,1,0:T(8,128)(2,1)} %copy.97), calls=%async_computation.1 | async-start | bytes 524288 | tf_op jit(solution)/shard_map/all_to_all | solution.py:144
  126.4 8.1 %all-to-all-done.1 = bf16[8,64,192]{2,1,0:T(8,128)(2,1)S(1)} async-done(((bf16[8,64,192]{2,1,0:T(8,128)(2,1)}), bf16[8,64,192]{2,1,0:T(8,128)(2,1)S(1)}, u32[]{:S(2)}, u32[]{:S(2)}) %all-to-all-start.1) | async-done | bytes 196640 | tf_op jit(solution)/shard_map/all_to_all | solution.py:144
  134.8 20.2 %all_gather.6 = bf16[8,64,768]{1,0,2:T(8,128)(2,1)} all-gather(bf16[8,64,192]{1,0,2:T(8,128)(2,1)S(1)} %copy.81), channel_id=1, replica_groups=mesh['ex'=8,'tp'=4] {'tp'}, dimensions={2}, use_global_device_ids=true | all-gather | bytes 983040 | tf_op jit(solution)/shard_map/all_gather | solution.py:150
  154.9 2.0 copy.82
  157.0 1.2 gather_fusion.1
  158.6 2.4 multiply_reduce_fusion
  161.1 1.2 reshape.493
  163.3 3.4 all-to-all-start.3
  166.8 9.5 %all-to-all-done.3 = bf16[8,64,192]{2,1,0:T(8,128)(2,1)S(1)} async-done(((bf16[8,64,192]{2,1,0:T(8,128)(2,1)}), bf16[8,64,192]{2,1,0:T(8,128)(2,1)S(1)}, u32[]{:S(2)}, u32[]{:S(2)}) %all-to-all-start.3) | async-done | bytes 196640 | tf_op jit(solution)/shard_map/all_to_all | solution.py:188
  176.6 13.6 %all_gather.7 = bf16[8,64,768]{1,0,2:T(8,128)(2,1)} all-gather(bf16[8,64,192]{1,0,2:T(8,128)(2,1)S(1)} %copy.86), channel_id=1, replica_groups=mesh['ex'=8,'tp'=4] {'tp'}, dimensions={2}, use_global_device_ids=true | all-gather | bytes 983040 | tf_op jit(solution)/shard_map/all_gather | solution.py:189
  190.2 2.0 copy.87
  192.2 1.9 gather_fusion.3
  194.1 1.4 reshape.441
  195.5 1.7 reduce_sum.164
  197.3 1.5 multiply_reduce_fusion.2
  201.0 1.1 fusion.85
  205.6 1.1 fusion.89
  206.7 3.5 convolution_bitcast_fusion.1
  210.2 3.5 convolution_bitcast_fusion
  215.2 21.0 %all-reduce.10.cloned.1.call-done = bf16[128,768]{1,0:T(8,128)(2,1)} async-done(((bf16[128,768]{1,0:T(8,128)(2,1)}), bf16[128,768]{1,0:T(8,128)(2,1)}) %all-reduce.10.cloned.1.call-update) | async-done | bytes 196624 | tf_op jit(solution)/shard_map/psum | solution.py:244
  236.2 1.2 fusion.40
  237.4 40.3 %all-reduce.2 = (f32[768]{0:T(1024)}, f32[768]{0:T(1024)}, f32[32,3]{0,1:T(4,128)}, f32[768,8]{0,1:T(8,128)}) all-reduce(f32[768]{0:T(1024)S(1)} %get-tuple-element.16, f32[768]{0:T(1024)S(1)} %get-tuple-element.12, f32[32,3]{0,1:T(4,128)S(1)} %fusion.25, f32[768,8]{0,1:T(8,128)S(1)} %fusion.98), channel_id=1, replica_groups=mesh['ex'=8,'tp'=4] {'ex'}, use_global_device_ids=true, to_apply=%region_30.31 | all-reduce | flops 7776 | bytes 62208 | tf_op jit(solution)/shard_map/psum | solution.py:252
  277.6 1.8 fusion.37
  279.4 71.9 %all-reduce.12.cloned.1.call-done = (f32[768,192]{0,1:T(8,128)}, f32[768,192]{0,1:T(8,128)}, f32[768,192]{0,1:T(8,128)}, f32[192,768]{1,0:T(8,128)}) async-done(((f32[768,192]{0,1:T(8,128)}, f32[768,192]{0,1:T(8,128)}, f32[768,192]{0,1:T(8,128)}, f32[192,768]{1,0:T(8,128)}), (f32[768,192]{0,1:T(8,128)}, f32[768,192]{0,1:T(8,128)}, f32[768,192]{0,1:T(8,128)}, ...) | async-done | bytes 2359312 | tf_op jit(solution)/shard_map/psum | solution.py:252
  351.4 2.0 copy.106
  (185 shorter events, 25.4 us)
Async XLA Ops:
  7.2 80.8 %copy-start = (bf16[1,768,768]{2,1,0:T(8,128)(2,1)S(1)}, bf16[1,768,768]{2,1,0:T(8,128)(2,1)}, u32[]{:S(2)}) copy-start(bf16[1,768,768]{2,1,0:T(8,128)(2,1)} %param.26) | copy-start | bytes 3538948
  7.2 4.5 %copy-start.1 = (bf16[128,768]{1,0:T(8,128)(2,1)S(1)}, bf16[128,768]{1,0:T(8,128)(2,1)}, u32[]{:S(2)}) copy-start(bf16[128,768]{1,0:T(8,128)(2,1)} %param.14) | copy-start | bytes 589828
  7.2 4.5 %copy-start.26 = (f32[768]{0:T(1024)S(1)}, f32[768]{0:T(1024)}, u32[]{:S(2)}) copy-start(f32[768]{0:T(1024)} %param.21) | copy-start | bytes 9220
  7.2 4.5 %copy-start.16 = (bf16[768,192]{0,1:T(8,128)(2,1)S(1)}, bf16[768,192]{0,1:T(8,128)(2,1)}, u32[]{:S(2)}) copy-start(bf16[768,192]{0,1:T(8,128)(2,1)} %param.17) | copy-start | bytes 884740
  7.2 4.8 %copy-start.18 = (bf16[768,192]{0,1:T(8,128)(2,1)S(1)}, bf16[768,192]{0,1:T(8,128)(2,1)}, u32[]{:S(2)}) copy-start(bf16[768,192]{0,1:T(8,128)(2,1)} %param.18) | copy-start | bytes 884740
  7.2 5.1 %copy-start.45 = (s32[1,4]{1,0:T(1,128)S(1)}, s32[1,4]{1,0:T(1,128)}, u32[]{:S(2)}) copy-start(s32[1,4]{1,0:T(1,128)} %param.16) | copy-start | bytes 52
  7.3 43.1 %all-reduce.8.cloned.1.call-start = ((), (), s32[]{:S(2)}) async-start(), calls=%async_computation.6 | async-start | bytes 786432 | tf_op jit(solution)/shard_map/psum | solution.py:112
  7.4 5.3 %copy-start.27 = (s32[128,128]{1,0:T(8,128)}, s32[128,128]{1,0:T(8,128)S(1)}, u32[]{:S(2)}) copy-start(s32[128,128]{1,0:T(8,128)S(1)} %compare_select_fusion) | copy-start | bytes 196612
  8.7 4.1 %copy-start.35 = (f32[128]{0:T(128)}, f32[128]{0:T(128)S(1)}, u32[]{:S(2)}) copy-start(f32[128]{0:T(128)S(1)} %add_rsqrt_fusion.1) | copy-start | bytes 1540
  10.1 3.8 %copy-start.6 = (bf16[192,768]{1,0:T(8,128)(2,1)S(1)}, bf16[192,768]{1,0:T(8,128)(2,1)}, u32[]{:S(2)}) copy-start(bf16[192,768]{1,0:T(8,128)(2,1)} %param.20) | copy-start | bytes 884740
  11.7 3.2 copy-start.24
  11.7 3.2 copy-start.31
  12.0 4.1 %copy-start.20 = (bf16[128,192]{0,1:T(8,128)(2,1)}, bf16[128,192]{0,1:T(8,128)(2,1)S(1)}, u32[]{:S(2)}) copy-start(bf16[128,192]{0,1:T(8,128)(2,1)S(1)} %convolution_convert_fusion.5) | copy-start | bytes 147460
  12.4 39.1 %copy-start.22 = (bf16[128,192]{0,1:T(8,128)(2,1)}, bf16[128,192]{0,1:T(8,128)(2,1)S(1)}, u32[]{:S(2)}) copy-start(bf16[128,192]{0,1:T(8,128)(2,1)S(1)} %convolution_convert_fusion.4) | copy-start | bytes 147460
  13.0 39.0 %copy-start.30 = (f32[768]{0:T(1024)S(1)}, f32[768]{0:T(1024)}, u32[]{:S(2)}) copy-start(f32[768]{0:T(1024)} %param.22) | copy-start | bytes 9220
  16.6 2.0 copy-start.42
  55.6 5.6 %copy-start.4 = (bf16[128,768]{1,0:T(8,128)(2,1)S(1)}, bf16[128,768]{1,0:T(8,128)(2,1)}, u32[]{:S(2)}) copy-start(bf16[128,768]{1,0:T(8,128)(2,1)} %param.27) | copy-start | bytes 589828
  55.6 24.9 %all-to-all-start = ((bf16[8,64,768]{2,1,0:T(8,128)(2,1)}), bf16[8,64,768]{2,1,0:T(8,128)(2,1)}, u32[]{:S(2)}, u32[]{:S(2)}) async-start(bf16[8,64,768]{2,1,0:T(8,128)(2,1)} %bitcast.13), calls=%async_computation | async-start | bytes 1572864 | tf_op jit(solution)/shard_map/all_to_all | solution.py:134
  62.0 3.4 copy-start.37
  65.0 3.0 copy-start.11
  80.5 4.4 %copy-start.44 = (bf16[1,768,768]{2,1,0:T(8,128)(2,1)S(1)}, bf16[1,768,768]{2,1,0:T(8,128)(2,1)}, u32[]{:S(2)}) copy-start(bf16[1,768,768]{2,1,0:T(8,128)(2,1)} %param.25) | copy-start | bytes 3538948
  80.5 23.9 %all-to-all-start.2 = ((bf16[8,64,768]{2,1,0:T(8,128)(2,1)}), bf16[8,64,768]{2,1,0:T(8,128)(2,1)}, u32[]{:S(2)}, u32[]{:S(2)}) async-start(bf16[8,64,768]{2,1,0:T(8,128)(2,1)} %bitcast.25), calls=%async_computation.2 | async-start | bytes 1572864 | tf_op jit(solution)/shard_map/all_to_all | solution.py:169
  84.8 33.1 %reduce-scatter.7.cloned.1.call-start = ((), (), s32[]{:S(2)}) async-start(), calls=%async_computation.8 | async-start | bytes 983040
  93.6 67.4 %reduce-scatter.9.cloned.1.call-start = ((), (), s32[]{:S(2)}) async-start(), calls=%async_computation.9 | async-start | bytes 1966080
  116.5 9.1 %copy-start.5 = (bf16[128,768]{1,0:T(8,128)(2,1)S(1)}, bf16[128,768]{1,0:T(8,128)(2,1)}, u32[]{:S(2)}) copy-start(bf16[128,768]{1,0:T(8,128)(2,1)} %param.27) | copy-start | bytes 589828
  116.5 9.9 %copy-start.43 = (s32[256,1]{0,1:T(1,128)S(1)}, s32[256,1]{0,1:T(1,128)}, u32[]{:S(2)}) copy-start(s32[256,1]{0,1:T(1,128)} %copy-done.42) | copy-start | bytes 3076
  120.1 14.4 %all-to-all-start.1 = ((bf16[8,64,192]{2,1,0:T(8,128)(2,1)}), bf16[8,64,192]{2,1,0:T(8,128)(2,1)S(1)}, u32[]{:S(2)}, u32[]{:S(2)}) async-start(bf16[8,64,192]{2,1,0:T(8,128)(2,1)} %copy.97), calls=%async_computation.1 | async-start | bytes 524288 | tf_op jit(solution)/shard_map/all_to_all | solution.py:144
  157.0 1.6 copy-start.12
  158.6 8.2 %copy-start.34 = (f32[128]{0:T(128)S(1)}, f32[128]{0:T(128)}, u32[]{:S(2)}) copy-start(f32[128]{0:T(128)} %copy-done.33) | copy-start | bytes 1540
  158.6 8.2 %copy-start.39 = (f32[128]{0:T(128)S(1)}, f32[128]{0:T(128)}, u32[]{:S(2)}) copy-start(f32[128]{0:T(128)} %copy-done.38) | copy-start | bytes 1540
  158.6 8.2 %copy-start.32 = (s32[128,2]{0,1:T(2,128)S(1)}, s32[128,2]{0,1:T(2,128)}, u32[]{:S(2)}) copy-start(s32[128,2]{0,1:T(2,128)} %param.15) | copy-start | bytes 3076
  163.3 13.1 %all-to-all-start.3 = ((bf16[8,64,192]{2,1,0:T(8,128)(2,1)}), bf16[8,64,192]{2,1,0:T(8,128)(2,1)S(1)}, u32[]{:S(2)}, u32[]{:S(2)}) async-start(bf16[8,64,192]{2,1,0:T(8,128)(2,1)} %copy.99), calls=%async_computation.3 | async-start | bytes 524288 | tf_op jit(solution)/shard_map/all_to_all | solution.py:188
  166.7 69.5 %all-reduce.10.cloned.1.call-start = ((), (), s32[]{:S(2)}) async-start(), calls=%async_computation.7 | async-start | bytes 393216 | tf_op jit(solution)/shard_map/psum | solution.py:244
  194.1 3.1 copy-start.29
  194.1 3.1 copy-start.41
  197.3 2.4 copy-start.7
  198.9 1.5 copy-start.21
  199.6 1.4 copy-start.36
  200.2 2.0 copy-start.14
  200.8 3.5 copy-start.19
  202.2 2.4 copy-start.15
  205.5 145.8 %all-reduce.12.cloned.1.call-start = ((), (), s32[]{:S(2)}) async-start(), calls=%async_computation.10 | async-start | bytes 4718592 | tf_op jit(solution)/shard_map/psum | solution.py:252
  206.7 3.5 copy-start.47
  210.2 3.5 copy-start.3
  210.2 3.9 %copy-start.28 = (s32[128,128]{1,0:T(8,128)S(1)}, s32[128,128]{1,0:T(8,128)}, u32[]{:S(2)}) copy-start(s32[128,128]{1,0:T(8,128)} %copy-done.27) | copy-start | bytes 196612
  351.4 2.1 copy-start.10
  351.4 2.9 copy-start.9
  351.4 3.7 %copy-start.8 = (f32[192,768]{1,0:T(8,128)S(1)}, f32[192,768]{1,0:T(8,128)}, u32[]{:S(2)}) copy-start(f32[192,768]{1,0:T(8,128)} %get-tuple-element.44) | copy-start | bytes 1769476
  (11 other events, 9.7 us)
Sparse Core Ops, SparseCore 0:
  15.0 35.3 all-reduce.7
  93.7 24.1 reduce-scatter.6
  121.0 34.1 reduce-scatter.8
  205.6 30.5 all-reduce.9
  240.5 110.7 all-reduce.11
where the time goes:
time: 364 us; the launch traced here: 362 us
  waiting for transfers between devices  167 us (46%)
  blocking collectives  74 us (20%)
  local copies, waits for them, and re-layouts  42.2 us (12%)
  matrix products  31.6 us (9%)
  starting transfers between devices  19.3 us (5%)
  between operations  14.6 us (4%)
  other arithmetic  14 us (4%)
    psum x1, waiting for transfers between devices, shards(): lax.psum((grad_w_query, grad_w_key, grad_w_value, grad_w_attn_out, grad_g...  71.9 us
    psum x1, blocking collectives, shards(): lax.psum((grad_w_query, grad_w_key, grad_w_value, grad_w_attn_out, grad_g...  40.3 us
    psum x1, waiting for transfers between devices, shards(): residual = inputs_f + lax.psum(head_part, 'tp')  31.8 us
    unnamed x113, local copies, waits for them, and re-layouts  23.8 us
    psum x1, waiting for transfers between devices, shards(): lax.psum(input_part.astype(jnp.bfloat16), 'tp').astype(jnp.float32)  21 us
    all_gather x1, blocking collectives, shards(): lax.all_gather(returned, 'tp', axis=2, tiled=True)  20.2 us
    all_gather x1, blocking collectives, shards(): lax.all_gather(row_back, 'tp', axis=2, tiled=True)  13.6 us
    all_to_all x1, waiting for transfers between devices, shards(): lax.all_to_all(send_rows, 'ex', split_axis=0, concat_axis=0, tiled=True)  12.4 us
  transfers between devices with their start and end apart: 9, of which 8 were waited for; matrix products, arithmetic and copies ran while one was open for 14% of the time, Pallas kernels for 0%

commit v1 on v0

--- a/solution.py
+++ b/solution.py
@@ -86,7 +86,11 @@
         buckets[None] == jnp.arange(rel_bias.shape[0], dtype=jnp.int32)[:, None, None]
     ).astype(jnp.float32)
     bias_full = jnp.einsum("bij,bh->hij", one_hot, rel_bias, precision=highest)
-    seq_ends = jnp.cumsum(lengths[0])
+    seq_count = lengths.shape[1]
+    seq_order = jnp.arange(seq_count, dtype=jnp.int32)
+    seq_ends = jnp.sum(
+        jnp.where(seq_order[None, :] <= seq_order[:, None], lengths[0][None, :], 0), -1
+    )
     positions = jnp.arange(tok_rows, dtype=jnp.int32)
     segments = jnp.sum((positions[:, None] >= seq_ends[None, :]).astype(jnp.int32), -1)
     allowed = (segments[:, None] == segments[None, :]) & (positions[:, None] >= positions[None, :])
@@ -122,7 +126,14 @@
     gate_values = gate_exp / jnp.sum(gate_exp, -1, keepdims=True)
     pair_routes = routes.reshape(-1)
     pair_hot = (pair_routes[:, None] == expert_ids[None, :]).astype(jnp.int32)
-    slot_index = jnp.sum(pair_hot * jnp.cumsum(pair_hot, 0), -1) - 1
+    pair_order = jnp.arange(pair_count, dtype=jnp.int32)
+    slot_index = jnp.sum(
+        (
+            (pair_routes[:, None] == pair_routes[None, :])
+            & (pair_order[None, :] < pair_order[:, None])
+        ).astype(jnp.int32),
+        -1,
+    )
     pair_slots = pair_routes * capacity + slot_index
     members = (
         jnp.full((experts * capacity,), pair_count, jnp.int32)

time: 364 us -> 364 us (level)
  no operation moved by 1% of the time
where the time goes in v1:
time: 364 us; the launch traced here: 362 us
  waiting for transfers between devices  168 us (46%)
  blocking collectives  74 us (20%)
  local copies, waits for them, and re-layouts  41.8 us (11%)
  matrix products  31.6 us (9%)
  starting transfers between devices  19.3 us (5%)
  between operations  14.6 us (4%)
  other arithmetic  13.4 us (4%)
    psum x1, waiting for transfers between devices, shards(): lax.psum((grad_w_query, grad_w_key, grad_w_value, grad_w_attn_out, grad_g...  72 us
    psum x1, blocking collectives, shards(): lax.psum((grad_w_query, grad_w_key, grad_w_value, grad_w_attn_out, grad_g...  40.2 us
    psum x1, waiting for transfers between devices, shards(): residual = inputs_f + lax.psum(head_part, 'tp')  32.7 us
    unnamed x113, local copies, waits for them, and re-layouts  23.8 us
    psum x1, waiting for transfers between devices, shards(): lax.psum(input_part.astype(jnp.bfloat16), 'tp').astype(jnp.float32)  21 us
    all_gather x1, blocking collectives, shards(): lax.all_gather(returned, 'tp', axis=2, tiled=True)  20.2 us
    all_gather x1, blocking collectives, shards(): lax.all_gather(row_back, 'tp', axis=2, tiled=True)  13.6 us
    all_to_all x1, waiting for transfers between devices, shards(): lax.all_to_all(send_rows, 'ex', split_axis=0, concat_axis=0, tiled=True)  12.4 us
  transfers between devices with their start and end apart: 9, of which 8 were waited for; matrix products, arithmetic and copies ran while one was open for 14% of the time, Pallas kernels for 0%

profile of v1, /device:TPU:0, one launch (start us, length us, event | category | flops | bytes accessed | tf_op | source)
XLA Modules:
  0.0 362.4 jit_solution(8996711575034821394)
XLA Ops:
  7.4 1.2 fusion.41
  8.7 1.4 fusion.1
  10.3 1.4 convolution_convert_fusion.6
  15.6 1.4 scatter_custom_fusion
  17.6 32.7 %all-reduce.8.cloned.1.call-done = f32[128,768]{1,0:T(8,128)} async-done(((f32[128,768]{1,0:T(8,128)}), f32[128,768]{1,0:T(8,128)}) %all-reduce.8.cloned.1.call-update) | async-done | bytes 393232 | tf_op jit(solution)/shard_map/psum | solution.py:116
  50.4 1.1 multiply_reduce_fusion.4
  52.8 2.7 gather_fusion
  55.5 5.6 %all-to-all-start = ((bf16[8,64,768]{2,1,0:T(8,128)(2,1)}), bf16[8,64,768]{2,1,0:T(8,128)(2,1)}, u32[]{:S(2)}, u32[]{:S(2)}) async-start(bf16[8,64,768]{2,1,0:T(8,128)(2,1)} %bitcast.10), calls=%async_computation | async-start | bytes 1572864 | tf_op jit(solution)/shard_map/all_to_all | solution.py:145
  65.3 2.7 gather_fusion.2
  68.0 12.4 %all-to-all-done = bf16[8,64,768]{2,1,0:T(8,128)(2,1)} async-done(((bf16[8,64,768]{2,1,0:T(8,128)(2,1)}), bf16[8,64,768]{2,1,0:T(8,128)(2,1)}, u32[]{:S(2)}, u32[]{:S(2)}) %all-to-all-start) | async-done | bytes 786464 | tf_op jit(solution)/shard_map/all_to_all | solution.py:145
  80.4 4.4 %all-to-all-start.2 = ((bf16[8,64,768]{2,1,0:T(8,128)(2,1)}), bf16[8,64,768]{2,1,0:T(8,128)(2,1)}, u32[]{:S(2)}, u32[]{:S(2)}) async-start(bf16[8,64,768]{2,1,0:T(8,128)(2,1)} %bitcast.22), calls=%async_computation.2 | async-start | bytes 1572864 | tf_op jit(solution)/shard_map/all_to_all | solution.py:180
  84.9 1.9 fusion.18
  86.8 1.1 copy-done.46
  87.9 2.0 convolution_convert_fusion
  89.9 2.0 copy.92
  91.9 1.7 reshape.444
  93.8 10.5 %all-to-all-done.2 = bf16[8,64,768]{2,1,0:T(8,128)(2,1)} async-done(((bf16[8,64,768]{2,1,0:T(8,128)(2,1)}), bf16[8,64,768]{2,1,0:T(8,128)(2,1)}, u32[]{:S(2)}, u32[]{:S(2)}) %all-to-all-start.2) | async-done | bytes 786464 | tf_op jit(solution)/shard_map/all_to_all | solution.py:180
  104.3 3.1 fusion.13
  108.3 2.1 fusion.16
  110.4 2.3 copy.94
  112.7 3.7 %reshape.446 = f32[768,512]{1,0:T(8,128)} reshape(f32[768,8,64]{2,1,0:T(8,128)} %bitcast.142) | data formatting | bytes 3145728
  116.5 1.4 reduce-scatter.7.cloned.1.call-done
  117.9 1.2 reshape.445
  120.1 5.5 %all-to-all-start.1 = ((bf16[8,64,192]{2,1,0:T(8,128)(2,1)}), bf16[8,64,192]{2,1,0:T(8,128)(2,1)S(1)}, u32[]{:S(2)}, u32[]{:S(2)}) async-start(bf16[8,64,192]{2,1,0:T(8,128)(2,1)} %copy.93), calls=%async_computation.1 | async-start | bytes 524288 | tf_op jit(solution)/shard_map/all_to_all | solution.py:155
  126.4 8.1 %all-to-all-done.1 = bf16[8,64,192]{2,1,0:T(8,128)(2,1)S(1)} async-done(((bf16[8,64,192]{2,1,0:T(8,128)(2,1)}), bf16[8,64,192]{2,1,0:T(8,128)(2,1)S(1)}, u32[]{:S(2)}, u32[]{:S(2)}) %all-to-all-start.1) | async-done | bytes 196640 | tf_op jit(solution)/shard_map/all_to_all | solution.py:155
  134.8 20.2 %all_gather.6 = bf16[8,64,768]{1,0,2:T(8,128)(2,1)} all-gather(bf16[8,64,192]{1,0,2:T(8,128)(2,1)S(1)} %copy.77), channel_id=1, replica_groups=mesh['ex'=8,'tp'=4] {'tp'}, dimensions={2}, use_global_device_ids=true | all-gather | bytes 983040 | tf_op jit(solution)/shard_map/all_gather | solution.py:161
  154.9 2.0 copy.78
  157.0 1.2 gather_fusion.1
  158.6 2.4 multiply_reduce_fusion
  161.0 1.2 reshape.447
  163.3 3.4 all-to-all-start.3
  166.8 9.5 %all-to-all-done.3 = bf16[8,64,192]{2,1,0:T(8,128)(2,1)S(1)} async-done(((bf16[8,64,192]{2,1,0:T(8,128)(2,1)}), bf16[8,64,192]{2,1,0:T(8,128)(2,1)S(1)}, u32[]{:S(2)}, u32[]{:S(2)}) %all-to-all-start.3) | async-done | bytes 196640 | tf_op jit(solution)/shard_map/all_to_all | solution.py:199
  176.6 13.6 %all_gather.7 = bf16[8,64,768]{1,0,2:T(8,128)(2,1)} all-gather(bf16[8,64,192]{1,0,2:T(8,128)(2,1)S(1)} %copy.82), channel_id=1, replica_groups=mesh['ex'=8,'tp'=4] {'tp'}, dimensions={2}, use_global_device_ids=true | all-gather | bytes 983040 | tf_op jit(solution)/shard_map/all_gather | solution.py:200
  190.2 2.0 copy.83
  192.2 1.9 gather_fusion.3
  194.1 1.4 reshape.395
  195.5 1.7 reduce_sum.177
  197.3 1.5 multiply_reduce_fusion.2
  201.0 1.1 fusion.84
  205.6 1.1 fusion.88
  206.7 3.5 convolution_bitcast_fusion.1
  210.2 3.5 convolution_bitcast_fusion
  215.2 21.0 %all-reduce.10.cloned.1.call-done = bf16[128,768]{1,0:T(8,128)(2,1)} async-done(((bf16[128,768]{1,0:T(8,128)(2,1)}), bf16[128,768]{1,0:T(8,128)(2,1)}) %all-reduce.10.cloned.1.call-update) | async-done | bytes 196624 | tf_op jit(solution)/shard_map/psum | solution.py:255
  236.2 1.2 fusion.40
  237.4 40.2 %all-reduce.2 = (f32[768]{0:T(1024)}, f32[768]{0:T(1024)}, f32[32,3]{0,1:T(4,128)}, f32[768,8]{0,1:T(8,128)}) all-reduce(f32[768]{0:T(1024)S(1)} %get-tuple-element.16, f32[768]{0:T(1024)S(1)} %get-tuple-element.12, f32[32,3]{0,1:T(4,128)S(1)} %fusion.25, f32[768,8]{0,1:T(8,128)S(1)} %fusion.97), channel_id=1, replica_groups=mesh['ex'=8,'tp'=4] {'ex'}, use_global_device_ids=true, to_apply=%region_28.29 | all-reduce | flops 7776 | bytes 62208 | tf_op jit(solution)/shard_map/psum | solution.py:263
  277.6 1.8 fusion.37
  279.4 72.0 %all-reduce.12.cloned.1.call-done = (f32[768,192]{0,1:T(8,128)}, f32[768,192]{0,1:T(8,128)}, f32[768,192]{0,1:T(8,128)}, f32[192,768]{1,0:T(8,128)}) async-done(((f32[768,192]{0,1:T(8,128)}, f32[768,192]{0,1:T(8,128)}, f32[768,192]{0,1:T(8,128)}, f32[192,768]{1,0:T(8,128)}), (f32[768,192]{0,1:T(8,128)}, f32[768,192]{0,1:T(8,128)}, f32[768,192]{0,1:T(8,128)}, ...) | async-done | bytes 2359312 | tf_op jit(solution)/shard_map/psum | solution.py:263
  351.4 2.0 copy.102
  (178 shorter events, 24.4 us)
Async XLA Ops:
  7.2 80.7 %copy-start = (bf16[1,768,768]{2,1,0:T(8,128)(2,1)S(1)}, bf16[1,768,768]{2,1,0:T(8,128)(2,1)}, u32[]{:S(2)}) copy-start(bf16[1,768,768]{2,1,0:T(8,128)(2,1)} %param.26) | copy-start | bytes 3538948
  7.2 4.5 %copy-start.1 = (bf16[128,768]{1,0:T(8,128)(2,1)S(1)}, bf16[128,768]{1,0:T(8,128)(2,1)}, u32[]{:S(2)}) copy-start(bf16[128,768]{1,0:T(8,128)(2,1)} %param.14) | copy-start | bytes 589828
  7.2 4.5 %copy-start.26 = (f32[768]{0:T(1024)S(1)}, f32[768]{0:T(1024)}, u32[]{:S(2)}) copy-start(f32[768]{0:T(1024)} %param.21) | copy-start | bytes 9220
  7.2 4.5 %copy-start.16 = (bf16[768,192]{0,1:T(8,128)(2,1)S(1)}, bf16[768,192]{0,1:T(8,128)(2,1)}, u32[]{:S(2)}) copy-start(bf16[768,192]{0,1:T(8,128)(2,1)} %param.17) | copy-start | bytes 884740
  7.2 4.8 %copy-start.18 = (bf16[768,192]{0,1:T(8,128)(2,1)S(1)}, bf16[768,192]{0,1:T(8,128)(2,1)}, u32[]{:S(2)}) copy-start(bf16[768,192]{0,1:T(8,128)(2,1)} %param.18) | copy-start | bytes 884740
  7.2 5.1 %copy-start.45 = (s32[1,4]{1,0:T(1,128)S(1)}, s32[1,4]{1,0:T(1,128)}, u32[]{:S(2)}) copy-start(s32[1,4]{1,0:T(1,128)} %param.16) | copy-start | bytes 52
  7.3 43.1 %all-reduce.8.cloned.1.call-start = ((), (), s32[]{:S(2)}) async-start(), calls=%async_computation.6 | async-start | bytes 786432 | tf_op jit(solution)/shard_map/psum | solution.py:116
  7.4 5.3 %copy-start.27 = (s32[128,128]{1,0:T(8,128)}, s32[128,128]{1,0:T(8,128)S(1)}, u32[]{:S(2)}) copy-start(s32[128,128]{1,0:T(8,128)S(1)} %compare_select_fusion) | copy-start | bytes 196612
  8.7 4.0 %copy-start.35 = (f32[128]{0:T(128)}, f32[128]{0:T(128)S(1)}, u32[]{:S(2)}) copy-start(f32[128]{0:T(128)S(1)} %add_rsqrt_fusion.1) | copy-start | bytes 1540
  10.1 3.8 %copy-start.6 = (bf16[192,768]{1,0:T(8,128)(2,1)S(1)}, bf16[192,768]{1,0:T(8,128)(2,1)}, u32[]{:S(2)}) copy-start(bf16[192,768]{1,0:T(8,128)(2,1)} %param.20) | copy-start | bytes 884740
  11.7 1.4 copy-start.24
  11.7 3.2 copy-start.31
  12.4 39.1 %copy-start.22 = (bf16[128,192]{0,1:T(8,128)(2,1)}, bf16[128,192]{0,1:T(8,128)(2,1)S(1)}, u32[]{:S(2)}) copy-start(bf16[128,192]{0,1:T(8,128)(2,1)S(1)} %convolution_convert_fusion.4) | copy-start | bytes 147460
  13.0 39.0 %copy-start.30 = (f32[768]{0:T(1024)S(1)}, f32[768]{0:T(1024)}, u32[]{:S(2)}) copy-start(f32[768]{0:T(1024)} %param.22) | copy-start | bytes 9220
  15.6 2.0 copy-start.42
  55.5 5.6 %copy-start.4 = (bf16[128,768]{1,0:T(8,128)(2,1)S(1)}, bf16[128,768]{1,0:T(8,128)(2,1)}, u32[]{:S(2)}) copy-start(bf16[128,768]{1,0:T(8,128)(2,1)} %param.27) | copy-start | bytes 589828
  55.5 24.9 %all-to-all-start = ((bf16[8,64,768]{2,1,0:T(8,128)(2,1)}), bf16[8,64,768]{2,1,0:T(8,128)(2,1)}, u32[]{:S(2)}, u32[]{:S(2)}) async-start(bf16[8,64,768]{2,1,0:T(8,128)(2,1)} %bitcast.10), calls=%async_computation | async-start | bytes 1572864 | tf_op jit(solution)/shard_map/all_to_all | solution.py:145
  61.9 3.4 copy-start.37
  65.0 3.0 copy-start.11
  80.4 4.4 %copy-start.44 = (bf16[1,768,768]{2,1,0:T(8,128)(2,1)S(1)}, bf16[1,768,768]{2,1,0:T(8,128)(2,1)}, u32[]{:S(2)}) copy-start(bf16[1,768,768]{2,1,0:T(8,128)(2,1)} %param.25) | copy-start | bytes 3538948
  80.4 23.9 %all-to-all-start.2 = ((bf16[8,64,768]{2,1,0:T(8,128)(2,1)}), bf16[8,64,768]{2,1,0:T(8,128)(2,1)}, u32[]{:S(2)}, u32[]{:S(2)}) async-start(bf16[8,64,768]{2,1,0:T(8,128)(2,1)} %bitcast.22), calls=%async_computation.2 | async-start | bytes 1572864 | tf_op jit(solution)/shard_map/all_to_all | solution.py:180
  84.8 33.1 %reduce-scatter.7.cloned.1.call-start = ((), (), s32[]{:S(2)}) async-start(), calls=%async_computation.8 | async-start | bytes 983040
  93.6 67.4 %reduce-scatter.9.cloned.1.call-start = ((), (), s32[]{:S(2)}) async-start(), calls=%async_computation.9 | async-start | bytes 1966080
  116.4 9.2 %copy-start.5 = (bf16[128,768]{1,0:T(8,128)(2,1)S(1)}, bf16[128,768]{1,0:T(8,128)(2,1)}, u32[]{:S(2)}) copy-start(bf16[128,768]{1,0:T(8,128)(2,1)} %param.27) | copy-start | bytes 589828
  116.5 9.9 %copy-start.43 = (s32[256,1]{0,1:T(1,128)S(1)}, s32[256,1]{0,1:T(1,128)}, u32[]{:S(2)}) copy-start(s32[256,1]{0,1:T(1,128)} %copy-done.42) | copy-start | bytes 3076
  120.1 14.4 %all-to-all-start.1 = ((bf16[8,64,192]{2,1,0:T(8,128)(2,1)}), bf16[8,64,192]{2,1,0:T(8,128)(2,1)S(1)}, u32[]{:S(2)}, u32[]{:S(2)}) async-start(bf16[8,64,192]{2,1,0:T(8,128)(2,1)} %copy.93), calls=%async_computation.1 | async-start | bytes 524288 | tf_op jit(solution)/shard_map/all_to_all | solution.py:155
  156.9 1.6 copy-start.12
  158.5 8.2 %copy-start.34 = (f32[128]{0:T(128)S(1)}, f32[128]{0:T(128)}, u32[]{:S(2)}) copy-start(f32[128]{0:T(128)} %copy-done.33) | copy-start | bytes 1540
  158.6 8.2 %copy-start.39 = (f32[128]{0:T(128)S(1)}, f32[128]{0:T(128)}, u32[]{:S(2)}) copy-start(f32[128]{0:T(128)} %copy-done.38) | copy-start | bytes 1540
  158.6 8.2 %copy-start.32 = (s32[128,2]{0,1:T(2,128)S(1)}, s32[128,2]{0,1:T(2,128)}, u32[]{:S(2)}) copy-start(s32[128,2]{0,1:T(2,128)} %param.15) | copy-start | bytes 3076
  163.3 13.1 %all-to-all-start.3 = ((bf16[8,64,192]{2,1,0:T(8,128)(2,1)}), bf16[8,64,192]{2,1,0:T(8,128)(2,1)S(1)}, u32[]{:S(2)}, u32[]{:S(2)}) async-start(bf16[8,64,192]{2,1,0:T(8,128)(2,1)} %copy.95), calls=%async_computation.3 | async-start | bytes 524288 | tf_op jit(solution)/shard_map/all_to_all | solution.py:199
  166.7 69.5 %all-reduce.10.cloned.1.call-start = ((), (), s32[]{:S(2)}) async-start(), calls=%async_computation.7 | async-start | bytes 393216 | tf_op jit(solution)/shard_map/psum | solution.py:255
  194.1 3.1 copy-start.29
  194.1 3.1 copy-start.41
  197.3 2.4 copy-start.7
  198.8 1.4 copy-start.23
  198.9 1.5 copy-start.21
  199.6 1.4 copy-start.36
  200.1 2.0 copy-start.14
  200.8 3.5 copy-start.19
  202.2 2.4 copy-start.15
  205.5 145.8 %all-reduce.12.cloned.1.call-start = ((), (), s32[]{:S(2)}) async-start(), calls=%async_computation.10 | async-start | bytes 4718592 | tf_op jit(solution)/shard_map/psum | solution.py:263
  206.7 3.5 copy-start.47
  210.2 3.5 copy-start.3
  210.2 3.9 %copy-start.28 = (s32[128,128]{1,0:T(8,128)S(1)}, s32[128,128]{1,0:T(8,128)}, u32[]{:S(2)}) copy-start(s32[128,128]{1,0:T(8,128)} %copy-done.27) | copy-start | bytes 196612
  351.4 2.1 copy-start.10
  351.4 2.9 copy-start.9
  351.4 3.7 %copy-start.8 = (f32[192,768]{1,0:T(8,128)S(1)}, f32[192,768]{1,0:T(8,128)}, u32[]{:S(2)}) copy-start(f32[192,768]{1,0:T(8,128)} %get-tuple-element.44) | copy-start | bytes 1769476
  (11 other events, 9.4 us)
Sparse Core Ops, SparseCore 0:
  15.0 35.3 all-reduce.7
  93.7 24.1 reduce-scatter.6
  121.0 34.1 reduce-scatter.8
  205.6 30.4 all-reduce.9
  240.5 110.7 all-reduce.11

commit v2 on v1

--- a/solution.py
+++ b/solution.py
@@ -4,6 +4,8 @@
 import jax
 import jax.numpy as jnp
 from jax import lax
+from jax.experimental import pallas as pl
+from jax.experimental.pallas import tpu as pltpu
 from jax.sharding import PartitionSpec as P
 
 eps = 1e-06
@@ -34,6 +36,254 @@
 def contract_cols(left_side, right_side):
     return lax.dot_general(
         left_side, right_side, (((1,), (1,)), ((), ())), preferred_element_type=jnp.float32
+    )
+
+
+VMEM_BYTES = 48 * 2**20
+
+
+def flip(index, bit):
+    return index + bit * (1 - 2 * ((index // bit) % 2))
+
+
+def flip_all(index, offset):
+    bit = 1
+    while bit <= offset:
+        if offset & bit:
+            index = flip(index, bit)
+        bit *= 2
+    return index
+
+
+def bits_of(count):
+    bits = []
+    bit = count // 2
+    while bit:
+        bits.append(bit)
+        bit //= 2
+    return bits
+
+
+def remote(src, dst, send_sem, recv_sem, axis, peer):
+    return pltpu.make_async_remote_copy(
+        src_ref=src,
+        dst_ref=dst,
+        send_sem=send_sem,
+        recv_sem=recv_sem,
+        device_id={axis: peer},
+        device_id_type=pl.DeviceIdType.MESH,
+    )
+
+
+def greet(partners):
+    barrier = pltpu.get_barrier_semaphore()
+    for axis, peer in partners:
+        pl.semaphore_signal(
+            barrier, inc=1, device_id={axis: peer}, device_id_type=pl.DeviceIdType.MESH
+        )
+    pl.semaphore_wait(barrier, len(partners))
+
+
+def all_peers(axis, count):
+    me = lax.axis_index(axis)
+    return [(axis, lax.rem(me + step, count)) for step in range(1, count)]
+
+
+def bit_peers(axis, count):
+    me = lax.axis_index(axis)
+    return [(axis, flip(me, bit)) for bit in bits_of(count)]
+
+
+def double_gather(axis, count, sets):
+    me = lax.axis_index(axis)
+    bits = bits_of(count)
+    sent = []
+
+    def send(offset, stage):
+        for bit in bits[stage:]:
+            for view, send_sems, recv_sems in sets:
+                block = view(flip_all(me, offset))
+                copy = remote(
+                    block,
+                    block,
+                    send_sems.at[offset ^ bit],
+                    recv_sems.at[offset ^ bit],
+                    axis,
+                    flip(me, bit),
+                )
+                copy.start()
+                sent.append(copy)
+
+    send(0, 0)
+    held = [0]
+    for stage, bit in enumerate(bits):
+        fresh = []
+        for offset in held:
+            arrived = offset ^ bit
+            for view, send_sems, recv_sems in sets:
+                block = view(flip_all(me, arrived))
+                remote(
+                    block, block, send_sems.at[arrived], recv_sems.at[arrived], axis, flip(me, bit)
+                ).wait_recv()
+            send(arrived, stage + 1)
+            fresh.append(arrived)
+        held = held + fresh
+    return sent
+
+
+def swap_blocks(axis, count, source, target, send_sems, recv_sems):
+    me = lax.axis_index(axis)
+    sent = []
+    for step in range(1, count):
+        peer = lax.rem(me + step, count)
+        copy = remote(
+            source(peer), target(me), send_sems.at[step], recv_sems.at[step], axis, peer
+        )
+        copy.start()
+        sent.append(copy)
+    for step in range(1, count):
+        origin = lax.rem(me + count - step, count)
+        remote(
+            source(origin), target(origin), send_sems.at[step], recv_sems.at[step], axis, origin
+        ).wait_recv()
+    return sent
+
+
+def finish(sent):
+    for copy in sent:
+        copy.wait_send()
+
+
+def sum_kernel(axis, count, x_ref, out_ref, low_ref, got_ref, s1, r1, s2, r2):
+    me = lax.axis_index(axis)
+    rows = x_ref.shape[0] // count
+
+    def part(ref, index):
+        return ref.at[pl.ds(pl.multiple_of(index * rows, rows), rows)]
+
+    low_ref[...] = x_ref[...].astype(jnp.bfloat16)
+    greet(all_peers(axis, count))
+    first = swap_blocks(
+        axis, count, lambda i: part(low_ref, i), lambda i: got_ref.at[i], s1, r1
+    )
+    mine = pl.ds(pl.multiple_of(me * rows, rows), rows)
+    got_ref[me] = jnp.zeros(got_ref.shape[1:], jnp.bfloat16)
+    total = x_ref[mine, :].astype(jnp.float32)
+    for index in range(count):
+        total = total + got_ref[index].astype(jnp.float32)
+    out_ref[mine, :] = total.astype(jnp.bfloat16)
+    second = double_gather(axis, count, [(lambda i: part(out_ref, i), s2, r2)])
+    finish(first + second)
+
+
+def dispatch_kernel(ex, tp, x_ref, out_ref, s1, r1, s2, r2):
+    me = lax.axis_index("ex")
+    column = lax.axis_index("tp")
+    greet(all_peers("ex", ex) + bit_peers("tp", tp))
+    out_ref[column, me] = x_ref[me]
+    first = swap_blocks(
+        "ex", ex, lambda i: x_ref.at[i], lambda i: out_ref.at[column, i], s1, r1
+    )
+    second = double_gather("tp", tp, [(lambda i: out_ref.at[i], s2, r2)])
+    finish(first + second)
+
+
+def return_kernel(ex, tp, x_ref, out_ref, held_ref, got_ref, s1, r1, s2, r2):
+    me = lax.axis_index("ex")
+    column = lax.axis_index("tp")
+    greet(all_peers("ex", ex) + bit_peers("tp", tp))
+    sent = []
+    live = list(range(tp))
+    source = x_ref
+    for bit in reversed(bits_of(tp)):
+        leaving = [offset for offset in live if offset & bit]
+        for offset in leaving:
+            copy = remote(
+                source.at[flip_all(column, offset)],
+                got_ref.at[offset],
+                s1.at[offset],
+                r1.at[offset],
+                "tp",
+                flip(column, bit),
+            )
+            copy.start()
+            sent.append(copy)
+        for offset in leaving:
+            kept = flip_all(column, offset ^ bit)
+            remote(
+                source.at[kept], got_ref.at[offset], s1.at[offset], r1.at[offset], "tp", flip(column, bit)
+            ).wait_recv()
+            held_ref[kept] = (
+                source[kept].astype(jnp.float32) + got_ref[offset].astype(jnp.float32)
+            ).astype(jnp.bfloat16)
+        live = [offset for offset in live if not offset & bit]
+        source = held_ref
+    out_ref[me] = held_ref[column, me]
+    second = swap_blocks(
+        "ex", ex, lambda i: held_ref.at[column, i], lambda i: out_ref.at[i], s2, r2
+    )
+    finish(sent + second)
+
+
+def gather_kernel(axis, count, number, *refs):
+    me = lax.axis_index(axis)
+    ins, outs, sems = refs[:number], refs[number : 2 * number], refs[2 * number :]
+    greet(bit_peers(axis, count))
+    sets = []
+    for index in range(number):
+        out_ref = outs[index]
+        out_ref[me] = ins[index][...]
+        sets.append(
+            (lambda i, out_ref=out_ref: out_ref.at[i], sems[2 * index], sems[2 * index + 1])
+        )
+    finish(double_gather(axis, count, sets))
+
+
+def call_kernel(body, ident, out_shapes, scratch, *operands):
+    return pl.pallas_call(
+        body,
+        out_shape=out_shapes,
+        in_specs=[pl.BlockSpec(memory_space=pltpu.VMEM)] * len(operands),
+        out_specs=jax.tree.map(lambda _: pl.BlockSpec(memory_space=pltpu.VMEM), out_shapes),
+        scratch_shapes=scratch,
+        compiler_params=pltpu.CompilerParams(
+            collective_id=ident, has_side_effects=True, vmem_limit_bytes=VMEM_BYTES
+        ),
+    )(*operands)
+
+
+def sems(*counts):
+    return [pltpu.SemaphoreType.DMA((count,)) for count in counts]
+
+
+def low_shape(*shape):
+    return jax.ShapeDtypeStruct(shape, jnp.bfloat16)
+
+
+def sum_over_tp(values, ident):
+    count = lax.axis_size("tp")
+    rows, width = values.shape
+    return call_kernel(
+        partial(sum_kernel, "tp", count),
+        ident,
+        low_shape(rows, width),
+        [
+            pltpu.VMEM((rows, width), jnp.bfloat16),
+            pltpu.VMEM((count, rows // count, width), jnp.bfloat16),
+        ]
+        + sems(count, count, count, count),
+        values,
+    )
+
+
+def gather_blocks(axis, ident, *arrays):
+    count = lax.axis_size(axis)
+    return call_kernel(
+        partial(gather_kernel, axis, count, len(arrays)),
+        ident,
+        [low_shape(count, *array.shape) for array in arrays],
+        sems(*([count] * (2 * len(arrays)))),
+        *arrays,
     )
 
 
@@ -112,8 +362,10 @@
         .astype(jnp.bfloat16)
         .reshape(tok_rows, -1)
     )
+    all_attn_in = lax.all_gather(attn_in, "ex", axis=0, tiled=True)
+    all_mixed = lax.all_gather(mixed_heads, "ex", axis=0, tiled=True)
     head_part = jnp.dot(mixed_heads, w_attn_out, preferred_element_type=jnp.float32)
-    residual = inputs_f + lax.psum(head_part, "tp")
+    residual = inputs_f + sum_over_tp(head_part, 0).astype(jnp.float32)
     scale_m = rms_scale(residual)
     normed_m = residual * scale_m
     moe_in = (normed_m * gain_moe).astype(jnp.bfloat16)
@@ -135,81 +387,119 @@
         -1,
     )
     pair_slots = pair_routes * capacity + slot_index
-    members = (
-        jnp.full((experts * capacity,), pair_count, jnp.int32)
-        .at[pair_slots]
-        .set(jnp.arange(pair_count, dtype=jnp.int32))
-    )
-    padded = jnp.concatenate([moe_in, jnp.zeros((1, model_width), jnp.bfloat16)], 0)
-    send_rows = padded[members // 2].reshape(experts, capacity, model_width)
-    arrived = lax.all_to_all(send_rows, "ex", split_axis=0, concat_axis=0, tiled=True)
-    slot_count = arrived.shape[1]
-    grouped = arrived.reshape(ex_devices, local_experts, slot_count, model_width)
-    pre_act = jnp.einsum("slcd,ldf->slcf", grouped, w_in, preferred_element_type=jnp.float32)
-    act_low = jax.nn.gelu(pre_act, approximate=True).astype(jnp.bfloat16)
-    partial_out = jnp.einsum("slcf,lfd->slcd", act_low, w_out, preferred_element_type=jnp.float32)
-    partial_out = partial_out.reshape(ex_devices * local_experts, slot_count, model_width)
-    owned_rows = lax.psum_scatter(
-        partial_out.astype(jnp.bfloat16), "tp", scatter_dimension=2, tiled=True
-    )
-    returned = lax.all_to_all(owned_rows, "ex", split_axis=0, concat_axis=0, tiled=True)
-    returned, kept_rows, kept_pre = (
-        returned,
-        arrived,
-        pre_act.reshape(ex_devices * local_experts, slot_count, -1),
-    )
-    expert_out = lax.all_gather(returned, "tp", axis=2, tiled=True).reshape(
-        experts * capacity, model_width
-    )
-    pair_out = expert_out[pair_slots].reshape(tok_rows, 2, model_width).astype(jnp.float32)
-    result = residual + jnp.sum(gate_values[:, :, None] * pair_out, 1)
-    output = result.astype(jnp.bfloat16)
+    slot_total = experts * capacity
+    pair_cols = pair_slots.reshape(tok_rows, 2).T.reshape(1, pair_count)
+    slot_hot = (
+        jnp.arange(slot_total, dtype=jnp.int32)[:, None] == pair_cols
+    ).astype(jnp.bfloat16)
     grad_out = cotangent.astype(jnp.float32)
-    gate_grad = jnp.sum(grad_out[:, None, :] * pair_out, -1)
+    tp_devices = lax.axis_size("tp")
+    tp_index = lax.axis_index("tp")
+    share = 2 * model_width // tp_devices
+    half = tp_devices // 2
+    moe_pairs = jnp.concatenate([moe_in, moe_in], 0)
+    grad_pairs = jnp.concatenate(
+        [(gate_values[:, j : j + 1] * grad_out).astype(jnp.bfloat16) for j in range(2)], 0
+    )
+    pair_rows = lax.dynamic_slice_in_dim(
+        jnp.concatenate([moe_pairs, grad_pairs], 1), tp_index * share, share, 1
+    )
+    send_rows = (
+        jnp.dot(slot_hot, pair_rows, preferred_element_type=jnp.float32)
+        .astype(jnp.bfloat16)
+        .reshape(ex_devices, slot_total // ex_devices, share)
+    )
+    slots_here = slot_total // ex_devices
+    arrived = call_kernel(
+        partial(dispatch_kernel, ex_devices, tp_devices),
+        1,
+        low_shape(tp_devices, ex_devices, slots_here, share),
+        sems(ex_devices, ex_devices, tp_devices, tp_devices),
+        send_rows,
+    ).reshape(tp_devices, slot_total, share)
+    moe_rows = jnp.concatenate([arrived[i] for i in range(half)], 1)
+    grad_rows = jnp.concatenate([arrived[i] for i in range(half, tp_devices)], 1)
+    in_here, out_here = w_in[0], w_out[0]
+    pre_act = jnp.dot(moe_rows, in_here, preferred_element_type=jnp.float32)
+    act_value, gelu_back = jax.vjp(partial(jax.nn.gelu, approximate=True), pre_act)
+    act_low = act_value.astype(jnp.bfloat16)
+    act_grad = contract_cols(grad_rows, out_here)
+    pre_grad = gelu_back(act_grad)[0].astype(jnp.bfloat16)
+    partial_out = jnp.dot(act_low, out_here, preferred_element_type=jnp.float32)
+    row_part = contract_cols(pre_grad, in_here)
+    back_rows = jnp.stack(
+        [
+            block[:, i * share : (i + 1) * share].astype(jnp.bfloat16)
+            for block in (partial_out, row_part)
+            for i in range(half)
+        ]
+    ).reshape(tp_devices, ex_devices, slots_here, share)
+    returned = call_kernel(
+        partial(return_kernel, ex_devices, tp_devices),
+        2,
+        low_shape(ex_devices, slots_here, share),
+        [
+            pltpu.VMEM((tp_devices, ex_devices, slots_here, share), jnp.bfloat16),
+            pltpu.VMEM((tp_devices, ex_devices, slots_here, share), jnp.bfloat16),
+        ]
+        + sems(tp_devices, tp_devices, ex_devices, ex_devices),
+        back_rows,
+    ).reshape(slot_total, share)
+    grad_w_out = contract_rows(act_low, grad_rows)[None]
+    grad_w_in = contract_rows(moe_rows, pre_grad)[None]
+    pair_back = contract_rows(slot_hot, returned)
+    is_out = tp_index < half
+    weights = jnp.where(is_out, gate_values, 1.0)
+    combined = (
+        weights[:, 0:1] * pair_back[:tok_rows] + weights[:, 1:2] * pair_back[tok_rows:]
+    )
+    grad_cols = lax.dynamic_slice_in_dim(grad_out, (tp_index % half) * share, share, 1)
+    gate_part = jnp.where(
+        is_out,
+        jnp.stack(
+            [
+                jnp.sum(grad_cols * pair_back[:tok_rows], -1),
+                jnp.sum(grad_cols * pair_back[tok_rows:], -1),
+            ],
+            1,
+        ),
+        0.0,
+    )
+    gate_high = gate_part.astype(jnp.bfloat16)
+    gate_low = (gate_part - gate_high.astype(jnp.float32)).astype(jnp.bfloat16)
+    [shared] = gather_blocks(
+        "tp",
+        3,
+        jnp.concatenate(
+            [
+                combined.astype(jnp.bfloat16),
+                gate_high,
+                gate_low,
+                jnp.zeros((tok_rows, 124), jnp.bfloat16),
+            ],
+            1,
+        ),
+    )
+    shared = shared.astype(jnp.float32)
+    output = (
+        residual + jnp.concatenate([shared[i, :, :share] for i in range(half)], 1)
+    ).astype(jnp.bfloat16)
+    row_sum = jnp.concatenate([shared[i, :, :share] for i in range(half, tp_devices)], 1)
+    gate_grad = jnp.sum(
+        shared[:, :, share : share + 2] + shared[:, :, share + 2 : share + 4], 0
+    )
     logit_pair = gate_values * (gate_grad - jnp.sum(gate_values * gate_grad, -1, keepdims=True))
     logit_grads = jnp.sum(logit_pair[:, :, None] * route_hot, 1)
-    grad_router = jnp.dot(moe_in.astype(jnp.float32).T, logit_grads, precision=highest)
-    moe_grad = jnp.dot(logit_grads, w_router.astype(jnp.float32).T, precision=highest)
-    pair_grads = (
-        (gate_values[:, :, None] * grad_out[:, None, :])
-        .astype(jnp.bfloat16)
-        .reshape(pair_count, model_width)
-    )
-    padded_grads = jnp.concatenate([pair_grads, jnp.zeros((1, model_width), jnp.bfloat16)], 0)
-    send_grad_rows = padded_grads[members].reshape(experts, capacity, model_width)
-    arrived_grads = lax.all_to_all(send_grad_rows, "ex", split_axis=0, concat_axis=0, tiled=True)
-    grad_group = arrived_grads.reshape(ex_devices, local_experts, capacity, model_width)
-    act_grad = jnp.einsum("slcd,lfd->slcf", grad_group, w_out, preferred_element_type=jnp.float32)
-    pre_keep = kept_pre.reshape(ex_devices, local_experts, capacity, -1)
-    act_value, gelu_back = jax.vjp(partial(jax.nn.gelu, approximate=True), pre_keep)
-    pre_grad = gelu_back(act_grad)[0].astype(jnp.bfloat16)
-    act_low = act_value.astype(jnp.bfloat16)
-    grad_w_out = jnp.einsum(
-        "slcf,slcd->lfd", act_low, grad_group, preferred_element_type=jnp.float32
-    )
-    rows_group = kept_rows.reshape(ex_devices, local_experts, capacity, model_width)
-    grad_w_in = jnp.einsum(
-        "slcd,slcf->ldf", rows_group, pre_grad, preferred_element_type=jnp.float32
-    )
-    row_part = jnp.einsum("slcf,ldf->slcd", pre_grad, w_in, preferred_element_type=jnp.float32)
-    row_part = row_part.reshape(ex_devices * local_experts, capacity, model_width)
-    row_share = lax.psum_scatter(row_part, "tp", scatter_dimension=2, tiled=True).astype(
-        jnp.bfloat16
-    )
-    row_back = lax.all_to_all(row_share, "ex", split_axis=0, concat_axis=0, tiled=True)
-    row_full = lax.all_gather(row_back, "tp", axis=2, tiled=True).reshape(
-        experts * capacity, model_width
-    )
-    moe_grad = moe_grad + jnp.sum(
-        row_full[pair_slots].reshape(tok_rows, 2, model_width).astype(jnp.float32), 1
-    )
+    router_rows = jnp.dot(logit_grads.T, moe_in.astype(jnp.float32), precision=highest)
+    moe_grad = row_sum + jnp.dot(logit_grads, w_router.astype(jnp.float32).T, precision=highest)
     grad_gain_moe = jnp.sum(moe_grad * normed_m, 0)
     normed_grad_m = moe_grad * gain_moe
     resid_grad = grad_out + scale_m * (
         normed_grad_m - normed_m * jnp.mean(normed_grad_m * normed_m, -1, keepdims=True)
     )
     attn_grad = resid_grad.astype(jnp.bfloat16)
-    grad_w_attn_out = contract_rows(mixed_heads, attn_grad)
+    all_attn_grad = lax.all_gather(attn_grad, "ex", axis=0, tiled=True)
+    grad_w_attn_out = contract_rows(all_mixed, all_attn_grad)
     mixed_grad = (
         contract_cols(attn_grad, w_attn_out)
         .astype(jnp.bfloat16)
@@ -244,15 +534,12 @@
         .reshape(tok_rows, -1)
     )
     value_flat = value_grad.reshape(tok_rows, -1)
-    grad_w_query = contract_rows(attn_in, query_grad)
-    grad_w_key = contract_rows(attn_in, key_grad)
-    grad_w_value = contract_rows(attn_in, value_flat)
     input_part = (
         contract_cols(query_grad, w_query)
         + contract_cols(key_grad, w_key)
         + contract_cols(value_flat, w_value)
     )
-    input_grad = lax.psum(input_part.astype(jnp.bfloat16), "tp").astype(jnp.float32)
+    input_grad = sum_over_tp(input_part, 4).astype(jnp.float32)
     grad_gain_attn = jnp.sum(input_grad * normed_a, 0)
     normed_grad_a = input_grad * gain_attn
     grad_inputs = (
@@ -260,30 +547,35 @@
         + scale_a
         * (normed_grad_a - normed_a * jnp.mean(normed_grad_a * normed_a, -1, keepdims=True))
     ).astype(jnp.bfloat16)
-    dense_sums = lax.psum(
-        (
-            grad_w_query,
-            grad_w_key,
-            grad_w_value,
-            grad_w_attn_out,
-            grad_gain_attn,
-            grad_gain_moe,
-            grad_rel_bias,
-            grad_router,
-        ),
-        "ex",
-    )
+    local_width = query_grad.shape[1]
+    buckets_count = rel_bias.shape[0]
+    flat_bias = grad_rel_bias.reshape(1, -1)
+    small_rows = jnp.concatenate(
+        [
+            grad_gain_attn[None],
+            grad_gain_moe[None],
+            router_rows,
+            jnp.pad(flat_bias, ((0, 0), (0, model_width - flat_bias.shape[1]))),
+        ],
+        0,
+    )
+    small_rows = jnp.pad(small_rows, ((0, -small_rows.shape[0] % 16), (0, 0)))
+    wide = jnp.concatenate([query_grad, key_grad, value_flat], 1)
+    wide = jnp.pad(wide, ((0, 0), (0, -wide.shape[1] % 128)))
+    all_wide, all_small = gather_blocks("ex", 5, wide, small_rows.astype(jnp.bfloat16))
+    projections = contract_rows(all_attn_in, all_wide.reshape(ex_devices * tok_rows, -1))
+    small_sum = jnp.sum(all_small.astype(jnp.float32), 0)
     return (
         output,
         grad_inputs,
-        dense_sums[0],
-        dense_sums[1],
-        dense_sums[2],
-        dense_sums[3],
-        dense_sums[4],
-        dense_sums[5],
-        dense_sums[6],
-        dense_sums[7],
+        projections[:, :local_width],
+        projections[:, local_width : 2 * local_width],
+        projections[:, 2 * local_width : 3 * local_width],
+        grad_w_attn_out,
+        small_sum[0],
+        small_sum[1],
+        small_sum[2 + experts, : buckets_count * local_heads].reshape(buckets_count, local_heads),
+        small_sum[2 : 2 + experts].T,
         grad_w_in,
         grad_w_out,
     )

time: 364 us -> 209 us (0.57)
  waiting for transfers between devices: 168 us -> 0.04 us
  Pallas kernels: 0 us -> 115 us
  blocking collectives: 74 us -> 28.2 us
  local copies, waits for them, and re-layouts: 41.8 us -> 14 us
  starting transfers between devices: 19.3 us -> 0.08 us
  matrix products: 31.6 us -> 26.4 us
  other arithmetic: 13.4 us -> 9.33 us
    psum x3 -> x0, waiting for transfers between devices: 126 us -> none  [the longest x1 72 us: shards(): lax.psum((grad_w_query, grad_w_key, grad_w_value, grad_w_attn_out, grad_g...]
    pallas_call x0 -> x6, Pallas kernels: none -> 115 us  [call_kernel(): pl.pallas_call(body, out_shape=out_shapes, in_specs=[pl.BlockSpec(memory_...]
    all_to_all x4 -> x0, waiting for transfers between devices: 40.5 us -> none  [the longest x1 12.4 us: shards(): lax.all_to_all(send_rows, 'ex', split_axis=0, concat_axis=0, tiled=True)]
    psum x1 -> x0, blocking collectives: 40.2 us -> none  [shards(): lax.psum((grad_w_query, grad_w_key, grad_w_value, grad_w_attn_out, grad_g...]
    unnamed x113 -> x82, local copies, waits for them, and re-layouts: 23.8 us -> 4.5 us
    all_to_all x4 -> x0, starting transfers between devices: 18.9 us -> none  [the longest x1 5.64 us: shards(): lax.all_to_all(send_rows, 'ex', split_axis=0, concat_axis=0, tiled=True)]
    dot_general x7 -> x4, matrix products: 16.3 us -> 3.03 us  [the longest x1 1.07 us: shards(): partial_out = jnp.dot(act_low, out_here, preferred_element_type=jnp.float32)]
    gather x4 -> x0, local copies, waits for them, and re-layouts: 8.55 us -> none  [the longest x1 2.71 us: shards(): padded_grads[members].reshape(experts, capacity, model_width)]
  transfers between devices with their start and end apart: 9 -> 2, of which waited for: 8 -> 0; matrix products, arithmetic and copies ran while one was open for 14% -> 19% of each run, Pallas kernels for 0% -> 55%
where the time goes in v2:
time: 209 us; the launch traced here: 208 us
  Pallas kernels  115 us (55%)
  blocking collectives  28.2 us (13%)
  matrix products  26.4 us (13%)
  between operations  14.8 us (7%)
  local copies, waits for them, and re-layouts  14 us (7%)
  other arithmetic  9.33 us (4%)
    pallas_call x6, Pallas kernels, call_kernel(): pl.pallas_call(body, out_shape=out_shapes, in_specs=[pl.BlockSpec(memory_...  115 us
    all_gather x1, blocking collectives, shards(): all_mixed = lax.all_gather(mixed_heads, 'ex', axis=0, tiled=True)  28.2 us
    dot_general x5, matrix products, contract_rows(): lax.dot_general(left_side, right_side, (((0,), (0,)), ((), ())), preferre...  11.8 us
    dot_general x6, matrix products, contract_cols(): lax.dot_general(left_side, right_side, (((1,), (1,)), ((), ())), preferre...  5.14 us
    unnamed x82, local copies, waits for them, and re-layouts  4.5 us
  transfers between devices with their start and end apart: 2, of which 0 were waited for; matrix products, arithmetic and copies ran while one was open for 19% of the time, Pallas kernels for 55%

profile of v2, /device:TPU:0, one launch (start us, length us, event | category | flops | bytes accessed | tf_op | source)
XLA Modules:
  0.0 208.2 jit_solution(11329750111953001687)
XLA Ops:
  7.3 1.1 fusion.37
  8.4 1.7 fusion.34
  10.4 1.3 convolution_convert_fusion.6
  11.7 1.5 fusion.1
  13.3 0.2 convolution_convert_fusion.7
  13.9 0.3 fusion.91
  14.3 0.2 convolution_convert_fusion.8
  14.7 0.4 copy-done.22
  15.1 0.2 fusion.92.x_ref
  15.4 10.9 %shard_map.229 = bf16[128,768]{1,0:T(8,128)(2,1)S(1)} custom-call(f32[128,768]{1,0:T(8,128)S(1)} %fusion.92.x_ref), custom_call_target="tpu_custom_call" | custom-call | tf_op jit(solution)/shard_map/pallas_call | solution.py:243
  28.1 1.0 convolution_convert_fusion.2
  29.1 22.8 %shard_map.230 = bf16[4,8,64,384]{3,2,1,0:T(8,128)(2,1)S(1)} custom-call(bf16[8,64,384]{2,1,0:T(8,128)(2,1)S(1)} %bitcast.108), custom_call_target="tpu_custom_call" | custom-call | tf_op jit(solution)/shard_map/pallas_call | solution.py:243
  52.2 1.4 copy-done.36
  53.6 0.8 fusion.15
  54.4 1.1 convolution_convert_fusion.1
  55.5 1.5 fusion.8
  57.0 0.8 convolution_convert_fusion
  58.0 0.8 fusion.89
  58.8 0.8 convert_element_type.287
  59.6 1.2 pad_maximum_fusion.x_ref
  60.8 29.7 %shard_map.231 = bf16[8,64,384]{2,1,0:T(8,128)(2,1)S(1)} custom-call(bf16[4,8,64,384]{3,2,1,0:T(8,128)(2,1)S(1)} %pad_maximum_fusion.x_ref), custom_call_target="tpu_custom_call" | custom-call | tf_op jit(solution)/shard_map/pallas_call | solution.py:243
  90.6 0.4 fusion.29
  91.6 6.1 %shard_map.232 = bf16[4,128,512]{2,1,0:T(8,128)(2,1)S(1)} custom-call(bf16[128,512]{1,0:T(8,128)(2,1)S(1)} %maximum_maximum_fusion.refs_0_), custom_call_target="tpu_custom_call" | custom-call | tf_op jit(solution)/shard_map/pallas_call | solution.py:243
  98.2 0.8 slice_bitcast_fusion.1
  99.1 0.5 multiply_reduce_fusion
  99.6 0.7 copy-done.5
  100.4 0.9 fusion.85
  101.3 1.2 convolution_convert_fusion.5
  102.5 0.3 multiply_reduce_fusion.3
  103.4 0.2 copy-done.19
  103.9 1.5 copy.135
  105.9 0.2 convolution_add_fusion.1
  106.2 1.2 convolution_add_fusion.x_ref
  107.4 9.4 %shard_map.233 = bf16[128,768]{1,0:T(8,128)(2,1)S(1)} custom-call(f32[128,768]{1,0:T(8,128)S(1)} %convolution_add_fusion.x_ref), custom_call_target="tpu_custom_call" | custom-call | tf_op jit(solution)/shard_map/pallas_call | solution.py:243
  116.8 1.1 fusion.22
  118.2 0.3 fusion.36
  118.6 36.4 %shard_map.234 = (bf16[8,128,640]{2,1,0:T(8,128)(2,1)S(1)}, bf16[8,16,768]{2,1,0:T(8,128)(2,1)S(1)}) custom-call(bf16[128,640]{1,0:T(8,128)(2,1)S(1)} %fusion.53.refs_0_, bf16[16,768]{1,0:T(8,128)(2,1)S(1)} %pad.16.refs_1_), custom_call_target="tpu_custom_call" | custom-call | tf_op jit(solution)/shard_map/pallas_call | solution.py:243
  155.0 0.6 copy-done.29
  155.8 0.7 copy.140
  156.4 1.4 slice_reduce_fusion.4
  157.9 28.2 %all_gather.10 = bf16[1024,192]{0,1:T(8,128)(2,1)} all-gather(bf16[128,192]{0,1:T(8,128)(2,1)S(1)} %bitcast.123), channel_id=1, replica_groups=mesh['ex'=8,'tp'=4] {'ex'}, dimensions={0}, use_global_device_ids=true | all-gather | bytes 442368 | tf_op jit(solution)/shard_map/all_gather | solution.py:366
  186.1 1.4 slice_bitcast_fusion.4
  187.5 3.7 %convolution_bitcast_fusion.1 = f32[1,768,768]{2,1,0:T(8,128)} fusion(bf16[512,768]{1,0:T(8,128)(2,1)} %copy-done.18, bf16[512,384]{1,0:T(8,128)(2,1)} %bitcast.115, bf16[512,384]{1,0:T(8,128)(2,1)} %bitcast.117), kind=kOutput, calls=%fused_computation.6 | convolution fusion | flops 605552640 | bytes 3932160 | tf_op jit(solution)/shard_map/dot_general | solution.py:31
  191.3 1.0 fusion.33
  192.4 2.3 %convolution_bitcast_fusion = f32[1,768,768]{2,1,0:T(8,128)} fusion(bf16[512,384]{1,0:T(8,128)(2,1)S(1)} %bitcast.137, bf16[512,384]{1,0:T(8,128)(2,1)S(1)} %bitcast.135, f32[512,768]{1,0:T(8,128)S(1)} %copy-done.39), kind=kOutput, calls=%fused_computation.5 | convolution fusion | flops 609091584 | bytes 4718592 | tf_op jit(solution)/shard_map/dot_general | solution.py:31
  194.7 2.7 %fusion.95 = f32[768,640]{0,1:T(8,128)S(1)} fusion(bf16[1024,768]{1,0:T(8,128)(2,1)} %all-gather.3.cloned.1.call-done, bf16[1024,640]{1,0:T(8,128)(2,1)S(1)} %bitcast.109), kind=kOutput, calls=%fused_computation.180 | convolution fusion | flops 1006632960 | bytes 4849664 | tf_op jit(solution)/shard_map/dot_general | solution.py:31
  197.4 1.2 fusion.87
  198.6 2.7 %fusion.96 = f32[192,768]{1,0:T(8,128)} fusion(bf16[1024,192]{0,1:T(8,128)(2,1)S(1)} %copy-done.4, bf16[1024,768]{1,0:T(8,128)(2,1)} %all-gather.5.cloned.1.call-done), kind=kOutput, calls=%fused_computation.181 | convolution fusion | flops 301989888 | bytes 2555904 | tf_op jit(solution)/shard_map/dot_general | solution.py:31
  (144 shorter events, 6.2 us)
Async XLA Ops:
  7.2 47.2 %copy-start = (bf16[1,768,768]{2,1,0:T(8,128)(2,1)S(1)}, bf16[1,768,768]{2,1,0:T(8,128)(2,1)}, u32[]{:S(2)}) copy-start(bf16[1,768,768]{2,1,0:T(8,128)(2,1)} %param.26) | copy-start | bytes 3538948
  7.2 6.1 %copy-start.11 = (bf16[768,192]{0,1:T(8,128)(2,1)S(1)}, bf16[768,192]{0,1:T(8,128)(2,1)}, u32[]{:S(2)}) copy-start(bf16[768,192]{0,1:T(8,128)(2,1)} %param.17) | copy-start | bytes 884740
  7.2 6.4 %copy-start.37 = (s32[1,4]{1,0:T(1,128)S(1)}, s32[1,4]{1,0:T(1,128)}, u32[]{:S(2)}) copy-start(s32[1,4]{1,0:T(1,128)} %param.16) | copy-start | bytes 52
  7.2 187.5 %all-gather.3.cloned.1.call-start = ((), (), s32[]{:S(2)}) async-start(), calls=%async_computation | async-start | bytes 1769472 | tf_op jit(solution)/shard_map/all_gather | solution.py:365
  10.1 3.2 %copy-start.2 = (bf16[128,768]{1,0:T(8,128)(2,1)S(1)}, bf16[128,768]{1,0:T(8,128)(2,1)}, u32[]{:S(2)}) copy-start(bf16[128,768]{1,0:T(8,128)(2,1)} %fusion.34) | copy-start | bytes 589828
  10.2 4.1 %copy-start.14 = (bf16[768,192]{0,1:T(8,128)(2,1)S(1)}, bf16[768,192]{0,1:T(8,128)(2,1)}, u32[]{:S(2)}) copy-start(bf16[768,192]{0,1:T(8,128)(2,1)} %param.19) | copy-start | bytes 884740
  10.2 188.5 %all-gather.5.cloned.1.call-start = ((), (), s32[]{:S(2)}) async-start(), calls=%async_computation.1 | async-start | bytes 1769472 | tf_op jit(solution)/shard_map/all_gather | solution.py:501
  10.3 3.6 %copy-start.30 = (s32[128,128]{1,0:T(8,128)}, s32[128,128]{1,0:T(8,128)S(1)}, u32[]{:S(2)}) copy-start(s32[128,128]{1,0:T(8,128)S(1)} %compare_select_fusion) | copy-start | bytes 196612
  11.7 3.5 %copy-start.9 = (bf16[192,768]{1,0:T(8,128)(2,1)S(1)}, bf16[192,768]{1,0:T(8,128)(2,1)}, u32[]{:S(2)}) copy-start(bf16[192,768]{1,0:T(8,128)(2,1)} %param.20) | copy-start | bytes 884740
  13.6 12.9 %copy-start.20 = (bf16[128,192]{0,1:T(8,128)(2,1)}, bf16[128,192]{0,1:T(8,128)(2,1)S(1)}, u32[]{:S(2)}) copy-start(bf16[128,192]{0,1:T(8,128)(2,1)S(1)} %convolution_convert_fusion.7) | copy-start | bytes 147460
  13.6 12.7 %copy-start.1 = (bf16[128,768]{1,0:T(8,128)(2,1)S(1)}, bf16[128,768]{1,0:T(8,128)(2,1)}, u32[]{:S(2)}) copy-start(bf16[128,768]{1,0:T(8,128)(2,1)} %param.14) | copy-start | bytes 589828
  13.9 12.6 %copy-start.34 = (s32[128,2]{0,1:T(2,128)S(1)}, s32[128,2]{0,1:T(2,128)}, u32[]{:S(2)}) copy-start(s32[128,2]{0,1:T(2,128)} %param.15) | copy-start | bytes 3076
  13.9 12.7 %copy-start.33 = (f32[768]{0:T(1024)S(1)}, f32[768]{0:T(1024)}, u32[]{:S(2)}) copy-start(f32[768]{0:T(1024)} %param.22) | copy-start | bytes 9220
  14.3 12.4 %copy-start.35 = (bf16[768,8]{0,1:T(8,128)(2,1)S(1)}, bf16[768,8]{0,1:T(8,128)(2,1)}, u32[]{:S(2)}) copy-start(bf16[768,8]{0,1:T(8,128)(2,1)} %param.24) | copy-start | bytes 36868
  14.5 0.6 copy-start.22
  15.1 12.8 %copy-start.3 = (bf16[128,768]{1,0:T(8,128)(2,1)S(1)}, bf16[128,768]{1,0:T(8,128)(2,1)}, u32[]{:S(2)}) copy-start(bf16[128,768]{1,0:T(8,128)(2,1)} %param.27) | copy-start | bytes 589828
  51.9 1.6 copy-start.36
  52.1 2.2 %copy-start.7 = (bf16[1,8,64,384]{3,2,1,0:T(8,128)(2,1)}, bf16[1,8,64,384]{3,2,1,0:T(8,128)(2,1)S(1)}, u32[]{:S(2)}) copy-start(bf16[1,8,64,384]{3,2,1,0:T(8,128)(2,1)S(1)} %get-tuple-element.109) | copy-start | bytes 1179652
  52.1 2.2 %copy-start.8 = (bf16[1,8,64,384]{3,2,1,0:T(8,128)(2,1)}, bf16[1,8,64,384]{3,2,1,0:T(8,128)(2,1)S(1)}, u32[]{:S(2)}) copy-start(bf16[1,8,64,384]{3,2,1,0:T(8,128)(2,1)S(1)} %get-tuple-element.110) | copy-start | bytes 1179652
  52.2 3.3 %copy-start.24 = (bf16[1,8,64,384]{3,2,1,0:T(8,128)(2,1)}, bf16[1,8,64,384]{3,2,1,0:T(8,128)(2,1)S(1)}, u32[]{:S(2)}) copy-start(bf16[1,8,64,384]{3,2,1,0:T(8,128)(2,1)S(1)} %get-tuple-element.107) | copy-start | bytes 1179652
  52.2 3.3 %copy-start.26 = (bf16[1,8,64,384]{3,2,1,0:T(8,128)(2,1)}, bf16[1,8,64,384]{3,2,1,0:T(8,128)(2,1)S(1)}, u32[]{:S(2)}) copy-start(bf16[1,8,64,384]{3,2,1,0:T(8,128)(2,1)S(1)} %get-tuple-element.108) | copy-start | bytes 1179652
  54.4 1.1 copy-start.38
  57.0 0.9 copy-start.18
  60.8 30.1 %copy-start.15 = (f32[128,768]{1,0:T(8,128)S(1)}, f32[128,768]{1,0:T(8,128)}, u32[]{:S(2)}) copy-start(f32[128,768]{1,0:T(8,128)} %convert_element_type.287) | copy-start | bytes 1179652
  99.1 2.2 %copy-start.10 = (bf16[192,768]{1,0:T(8,128)(2,1)S(1)}, bf16[192,768]{1,0:T(8,128)(2,1)}, u32[]{:S(2)}) copy-start(bf16[192,768]{1,0:T(8,128)(2,1)} %param.20) | copy-start | bytes 884740
  99.1 3.4 %copy-start.23 = (bf16[128,192]{0,1:T(8,128)(2,1)S(1)}, bf16[128,192]{0,1:T(8,128)(2,1)}, u32[]{:S(2)}) copy-start(bf16[128,192]{0,1:T(8,128)(2,1)} %copy-done.22) | copy-start | bytes 147460
  99.6 0.8 copy-start.5
  100.4 2.6 %copy-start.21 = (bf16[128,192]{0,1:T(8,128)(2,1)S(1)}, bf16[128,192]{0,1:T(8,128)(2,1)}, u32[]{:S(2)}) copy-start(bf16[128,192]{0,1:T(8,128)(2,1)} %copy-done.20) | copy-start | bytes 147460
  101.3 2.4 %copy-start.12 = (bf16[768,192]{0,1:T(8,128)(2,1)S(1)}, bf16[768,192]{0,1:T(8,128)(2,1)}, u32[]{:S(2)}) copy-start(bf16[768,192]{0,1:T(8,128)(2,1)} %param.17) | copy-start | bytes 884740
  102.8 3.1 %copy-start.13 = (bf16[768,192]{0,1:T(8,128)(2,1)S(1)}, bf16[768,192]{0,1:T(8,128)(2,1)}, u32[]{:S(2)}) copy-start(bf16[768,192]{0,1:T(8,128)(2,1)} %param.18) | copy-start | bytes 884740
  103.0 0.6 copy-start.19
  105.7 11.1 %copy-start.31 = (s32[128,128]{1,0:T(8,128)S(1)}, s32[128,128]{1,0:T(8,128)}, u32[]{:S(2)}) copy-start(s32[128,128]{1,0:T(8,128)} %copy-done.30) | copy-start | bytes 196612
  105.9 12.3 %copy-start.32 = (f32[768]{0:T(1024)S(1)}, f32[768]{0:T(1024)}, u32[]{:S(2)}) copy-start(f32[768]{0:T(1024)} %param.21) | copy-start | bytes 9220
  106.1 12.4 %copy-start.28 = (bf16[128,192]{1,0:T(8,128)(2,1)S(1)}, bf16[128,192]{1,0:T(8,128)(2,1)}, u32[]{:S(2)}) copy-start(bf16[128,192]{1,0:T(8,128)(2,1)} %copy.135) | copy-start | bytes 147460
  155.0 0.6 copy-start.29
  187.5 3.8 %copy-start.6 = (f32[128,768]{1,0:T(8,128)S(1)}, f32[128,768]{1,0:T(8,128)}, u32[]{:S(2)}) copy-start(f32[128,768]{1,0:T(8,128)} %copy-done.5) | copy-start | bytes 1179652
  187.5 3.8 %copy-start.16 = (f32[128,384]{1,0:T(8,128)S(1)}, f32[128,384]{1,0:T(8,128)}, u32[]{:S(2)}) copy-start(f32[128,384]{1,0:T(8,128)} %get-tuple-element.113) | copy-start | bytes 589828
  187.5 3.8 %copy-start.17 = (f32[128,384]{1,0:T(8,128)S(1)}, f32[128,384]{1,0:T(8,128)}, u32[]{:S(2)}) copy-start(f32[128,384]{1,0:T(8,128)} %get-tuple-element.114) | copy-start | bytes 589828
  187.5 4.8 %copy-start.39 = (f32[512,768]{1,0:T(8,128)S(1)}, f32[512,768]{1,0:T(8,128)}, u32[]{:S(2)}) copy-start(f32[512,768]{1,0:T(8,128)} %copy-done.38) | copy-start | bytes 4718596
  191.2 1.1 copy-start.25
  191.2 1.1 copy-start.27
  197.4 1.3 copy-start.4
Sparse Core Ops, SparseCore 0:
  10.3 47.3 all-gather.2
  101.4 55.0 all-gather.4

commit v3 on v2

--- a/solution.py
+++ b/solution.py
@@ -94,10 +94,9 @@
     return [(axis, flip(me, bit)) for bit in bits_of(count)]
 
 
-def double_gather(axis, count, sets):
+def double_gather(axis, count, sets, sent):
     me = lax.axis_index(axis)
     bits = bits_of(count)
-    sent = []
 
     def send(offset, stage):
         for bit in bits[stage:]:
@@ -115,6 +114,7 @@
                 sent.append(copy)
 
     send(0, 0)
+    yield
     held = [0]
     for stage, bit in enumerate(bits):
         fresh = []
@@ -128,10 +128,16 @@
             send(arrived, stage + 1)
             fresh.append(arrived)
         held = held + fresh
-    return sent
-
-
-def swap_blocks(axis, count, source, target, send_sems, recv_sems):
+        yield
+
+
+def in_turn(*flows):
+    flows = list(flows)
+    while flows:
+        flows = [flow for flow in flows if next(flow, 1) is None]
+
+
+def swap_blocks(axis, count, source, target, send_sems, recv_sems, between):
     me = lax.axis_index(axis)
     sent = []
     for step in range(1, count):
@@ -141,6 +147,7 @@
         )
         copy.start()
         sent.append(copy)
+    between()
     for step in range(1, count):
         origin = lax.rem(me + count - step, count)
         remote(
@@ -154,17 +161,41 @@
         copy.wait_send()
 
 
-def sum_kernel(axis, count, x_ref, out_ref, low_ref, got_ref, s1, r1, s2, r2):
-    me = lax.axis_index(axis)
+def sum_kernel(count, ex, number, *refs):
+    x_ref, extras = refs[0], refs[1 : 1 + number]
+    out_ref, extra_outs = refs[1 + number], refs[2 + number : 2 + 2 * number]
+    low_ref, got_ref, s1, r1, s2, r2 = refs[2 + 2 * number : 8 + 2 * number]
+    extra_sems = refs[8 + 2 * number :]
+    me = lax.axis_index("tp")
+    group = lax.axis_index("ex")
     rows = x_ref.shape[0] // count
 
     def part(ref, index):
         return ref.at[pl.ds(pl.multiple_of(index * rows, rows), rows)]
 
     low_ref[...] = x_ref[...].astype(jnp.bfloat16)
-    greet(all_peers(axis, count))
+    sets = []
+    for index in range(number):
+        extra_out = extra_outs[index]
+        extra_out[group] = extras[index][...]
+        sets.append(
+            (
+                lambda i, extra_out=extra_out: extra_out.at[i],
+                extra_sems[2 * index],
+                extra_sems[2 * index + 1],
+            )
+        )
+    greet(all_peers("tp", count) + bit_peers("ex", ex))
+    sent = []
+    wide_flow = double_gather("ex", ex, sets, sent)
     first = swap_blocks(
-        axis, count, lambda i: part(low_ref, i), lambda i: got_ref.at[i], s1, r1
+        "tp",
+        count,
+        lambda i: part(low_ref, i),
+        lambda i: got_ref.at[i],
+        s1,
+        r1,
+        lambda: next(wide_flow),
     )
     mine = pl.ds(pl.multiple_of(me * rows, rows), rows)
     got_ref[me] = jnp.zeros(got_ref.shape[1:], jnp.bfloat16)
@@ -172,20 +203,73 @@
     for index in range(count):
         total = total + got_ref[index].astype(jnp.float32)
     out_ref[mine, :] = total.astype(jnp.bfloat16)
-    second = double_gather(axis, count, [(lambda i: part(out_ref, i), s2, r2)])
-    finish(first + second)
+    in_turn(
+        double_gather("tp", count, [(lambda i: part(out_ref, i), s2, r2)], sent), wide_flow
+    )
+    finish(first + sent)
 
 
 def dispatch_kernel(ex, tp, x_ref, out_ref, s1, r1, s2, r2):
     me = lax.axis_index("ex")
     column = lax.axis_index("tp")
+    bits = bits_of(tp)
     greet(all_peers("ex", ex) + bit_peers("tp", tp))
     out_ref[column, me] = x_ref[me]
-    first = swap_blocks(
-        "ex", ex, lambda i: x_ref.at[i], lambda i: out_ref.at[column, i], s1, r1
-    )
-    second = double_gather("tp", tp, [(lambda i: out_ref.at[i], s2, r2)])
-    finish(first + second)
+    sent = []
+
+    def relay(offset, stage, step, origin):
+        for bit in bits[stage:]:
+            block = out_ref.at[flip_all(column, offset), origin]
+            copy = remote(
+                block,
+                block,
+                s2.at[offset ^ bit, step],
+                r2.at[offset ^ bit, step],
+                "tp",
+                flip(column, bit),
+            )
+            copy.start()
+            sent.append(copy)
+
+    for step in range(1, ex):
+        peer = lax.rem(me + step, ex)
+        copy = remote(
+            x_ref.at[peer], out_ref.at[column, me], s1.at[step], r1.at[step], "ex", peer
+        )
+        copy.start()
+        sent.append(copy)
+    for turn in range(ex + 2):
+        if turn < ex:
+            origin = lax.rem(me + ex - turn, ex)
+            if turn:
+                remote(
+                    x_ref.at[origin],
+                    out_ref.at[column, origin],
+                    s1.at[turn],
+                    r1.at[turn],
+                    "ex",
+                    origin,
+                ).wait_recv()
+            relay(0, 0, turn, origin)
+        if turn >= 2:
+            step = turn - 2
+            origin = lax.rem(me + ex - step, ex)
+            held = [0]
+            for stage, bit in enumerate(bits):
+                fresh = [offset ^ bit for offset in held]
+                for arrived in fresh:
+                    block = out_ref.at[flip_all(column, arrived), origin]
+                    remote(
+                        block,
+                        block,
+                        s2.at[arrived, step],
+                        r2.at[arrived, step],
+                        "tp",
+                        flip(column, bit),
+                    ).wait_recv()
+                    relay(arrived, stage + 1, step, origin)
+                held = held + fresh
+    finish(sent)
 
 
 def return_kernel(ex, tp, x_ref, out_ref, held_ref, got_ref, s1, r1, s2, r2):
@@ -193,50 +277,90 @@
     column = lax.axis_index("tp")
     greet(all_peers("ex", ex) + bit_peers("tp", tp))
     sent = []
+    stages = []
     live = list(range(tp))
-    source = x_ref
     for bit in reversed(bits_of(tp)):
-        leaving = [offset for offset in live if offset & bit]
-        for offset in leaving:
-            copy = remote(
-                source.at[flip_all(column, offset)],
-                got_ref.at[offset],
-                s1.at[offset],
-                r1.at[offset],
-                "tp",
-                flip(column, bit),
-            )
+        stages.append((bit, [offset for offset in live if offset & bit]))
+        live = [offset for offset in live if not offset & bit]
+    steps = list(range(1, ex)) + [0]
+
+    def hop(source, stage, offset, step, target):
+        return remote(
+            source.at[flip_all(column, offset), target],
+            got_ref.at[offset, target],
+            s1.at[offset, step],
+            r1.at[offset, step],
+            "tp",
+            flip(column, stages[stage][0]),
+        )
+
+    def send(source, stage, step, target):
+        for offset in stages[stage][1]:
+            copy = hop(source, stage, offset, step, target)
             copy.start()
             sent.append(copy)
-        for offset in leaving:
-            kept = flip_all(column, offset ^ bit)
-            remote(
-                source.at[kept], got_ref.at[offset], s1.at[offset], r1.at[offset], "tp", flip(column, bit)
-            ).wait_recv()
-            held_ref[kept] = (
-                source[kept].astype(jnp.float32) + got_ref[offset].astype(jnp.float32)
-            ).astype(jnp.bfloat16)
-        live = [offset for offset in live if not offset & bit]
+
+    for step in steps:
+        send(x_ref, 0, step, lax.rem(me + step, ex))
+    source = x_ref
+    for stage, (bit, leaving) in enumerate(stages):
+        for step in steps:
+            target = lax.rem(me + step, ex)
+            for offset in leaving:
+                hop(source, stage, offset, step, target).wait_recv()
+                kept = flip_all(column, offset ^ bit)
+                held_ref[kept, target] = (
+                    source[kept, target].astype(jnp.float32)
+                    + got_ref[offset, target].astype(jnp.float32)
+                ).astype(jnp.bfloat16)
+            if stage + 1 < len(stages):
+                send(held_ref, stage + 1, step, target)
+            elif step:
+                copy = remote(
+                    held_ref.at[column, target],
+                    out_ref.at[me],
+                    s2.at[step],
+                    r2.at[step],
+                    "ex",
+                    target,
+                )
+                copy.start()
+                sent.append(copy)
+            else:
+                out_ref[me] = held_ref[column, me]
         source = held_ref
-    out_ref[me] = held_ref[column, me]
-    second = swap_blocks(
-        "ex", ex, lambda i: held_ref.at[column, i], lambda i: out_ref.at[i], s2, r2
-    )
-    finish(sent + second)
-
-
-def gather_kernel(axis, count, number, *refs):
-    me = lax.axis_index(axis)
+    for step in range(1, ex):
+        origin = lax.rem(me + ex - step, ex)
+        remote(
+            held_ref.at[column, origin], out_ref.at[origin], s2.at[step], r2.at[step], "ex", origin
+        ).wait_recv()
+    finish(sent)
+
+
+def gather_kernel(plan, sizes, *refs):
+    number = len(plan)
     ins, outs, sems = refs[:number], refs[number : 2 * number], refs[2 * number :]
-    greet(bit_peers(axis, count))
-    sets = []
-    for index in range(number):
-        out_ref = outs[index]
-        out_ref[me] = ins[index][...]
-        sets.append(
-            (lambda i, out_ref=out_ref: out_ref.at[i], sems[2 * index], sems[2 * index + 1])
-        )
-    finish(double_gather(axis, count, sets))
+    axes = sorted(set(axis for axis, _ in plan))
+    greet([peer for axis in axes for peer in bit_peers(axis, sizes[axis])])
+    sent = []
+    flows = []
+    for axis in axes:
+        me = lax.axis_index(axis)
+        sets = []
+        for index in range(number):
+            if plan[index][0] != axis:
+                continue
+            out_ref = outs[index]
+            if plan[index][1]:
+                out_ref[:, me] = ins[index][...]
+                view = lambda i, out_ref=out_ref: out_ref.at[:, i]
+            else:
+                out_ref[me] = ins[index][...]
+                view = lambda i, out_ref=out_ref: out_ref.at[i]
+            sets.append((view, sems[2 * index], sems[2 * index + 1]))
+        flows.append(double_gather(axis, sizes[axis], sets, sent))
+    in_turn(*flows)
+    finish(sent)
 
 
 def call_kernel(body, ident, out_shapes, scratch, *operands):
@@ -253,37 +377,46 @@
 
 
 def sems(*counts):
-    return [pltpu.SemaphoreType.DMA((count,)) for count in counts]
+    return [
+        pltpu.SemaphoreType.DMA(count if isinstance(count, tuple) else (count,))
+        for count in counts
+    ]
 
 
 def low_shape(*shape):
     return jax.ShapeDtypeStruct(shape, jnp.bfloat16)
 
 
-def sum_over_tp(values, ident):
-    count = lax.axis_size("tp")
+def sum_over_tp(ident, values, *extras):
+    count, ex = lax.axis_size("tp"), lax.axis_size("ex")
     rows, width = values.shape
     return call_kernel(
-        partial(sum_kernel, "tp", count),
+        partial(sum_kernel, count, ex, len(extras)),
         ident,
-        low_shape(rows, width),
+        [low_shape(rows, width)] + [low_shape(ex, *extra.shape) for extra in extras],
         [
             pltpu.VMEM((rows, width), jnp.bfloat16),
             pltpu.VMEM((count, rows // count, width), jnp.bfloat16),
         ]
-        + sems(count, count, count, count),
+        + sems(count, count, count, count, *([ex] * (2 * len(extras)))),
         values,
-    )
-
-
-def gather_blocks(axis, ident, *arrays):
-    count = lax.axis_size(axis)
+        *extras,
+    )
+
+
+def gather_blocks(ident, plan, *arrays):
+    sizes = {axis: lax.axis_size(axis) for axis in ("ex", "tp")}
+    shapes = []
+    counts = []
+    for (axis, inner), array in zip(plan, arrays):
+        count = sizes[axis]
+        counts += [count, count]
+        if inner:
+            shapes.append(low_shape(array.shape[0], count, *array.shape[1:]))
+        else:
+            shapes.append(low_shape(count, *array.shape))
     return call_kernel(
-        partial(gather_kernel, axis, count, len(arrays)),
-        ident,
-        [low_shape(count, *array.shape) for array in arrays],
-        sems(*([count] * (2 * len(arrays)))),
-        *arrays,
+        partial(gather_kernel, plan, sizes), ident, shapes, sems(*counts), *arrays
     )
 
 
@@ -362,10 +495,18 @@
         .astype(jnp.bfloat16)
         .reshape(tok_rows, -1)
     )
-    all_attn_in = lax.all_gather(attn_in, "ex", axis=0, tiled=True)
-    all_mixed = lax.all_gather(mixed_heads, "ex", axis=0, tiled=True)
     head_part = jnp.dot(mixed_heads, w_attn_out, preferred_element_type=jnp.float32)
-    residual = inputs_f + sum_over_tp(head_part, 0).astype(jnp.float32)
+    tp_devices = lax.axis_size("tp")
+    tp_index = lax.axis_index("tp")
+    quarter = tok_rows // tp_devices
+
+    def own_quarter(rows):
+        return lax.dynamic_slice_in_dim(rows, tp_index * quarter, quarter, 0)
+
+    head_sum, quarter_in, all_mixed = sum_over_tp(
+        0, head_part, own_quarter(attn_in), mixed_heads
+    )
+    residual = inputs_f + head_sum.astype(jnp.float32)
     scale_m = rms_scale(residual)
     normed_m = residual * scale_m
     moe_in = (normed_m * gain_moe).astype(jnp.bfloat16)
@@ -393,8 +534,6 @@
         jnp.arange(slot_total, dtype=jnp.int32)[:, None] == pair_cols
     ).astype(jnp.bfloat16)
     grad_out = cotangent.astype(jnp.float32)
-    tp_devices = lax.axis_size("tp")
-    tp_index = lax.axis_index("tp")
     share = 2 * model_width // tp_devices
     half = tp_devices // 2
     moe_pairs = jnp.concatenate([moe_in, moe_in], 0)
@@ -414,7 +553,7 @@
         partial(dispatch_kernel, ex_devices, tp_devices),
         1,
         low_shape(tp_devices, ex_devices, slots_here, share),
-        sems(ex_devices, ex_devices, tp_devices, tp_devices),
+        sems(ex_devices, ex_devices, *[(tp_devices, ex_devices)] * 2),
         send_rows,
     ).reshape(tp_devices, slot_total, share)
     moe_rows = jnp.concatenate([arrived[i] for i in range(half)], 1)
@@ -442,7 +581,7 @@
             pltpu.VMEM((tp_devices, ex_devices, slots_here, share), jnp.bfloat16),
             pltpu.VMEM((tp_devices, ex_devices, slots_here, share), jnp.bfloat16),
         ]
-        + sems(tp_devices, tp_devices, ex_devices, ex_devices),
+        + sems(*[(tp_devices, ex_devices)] * 2, ex_devices, ex_devices),
         back_rows,
     ).reshape(slot_total, share)
     grad_w_out = contract_rows(act_low, grad_rows)[None]
@@ -468,8 +607,8 @@
     gate_high = gate_part.astype(jnp.bfloat16)
     gate_low = (gate_part - gate_high.astype(jnp.float32)).astype(jnp.bfloat16)
     [shared] = gather_blocks(
-        "tp",
         3,
+        (("tp", False),),
         jnp.concatenate(
             [
                 combined.astype(jnp.bfloat16),
@@ -498,8 +637,6 @@
         normed_grad_m - normed_m * jnp.mean(normed_grad_m * normed_m, -1, keepdims=True)
     )
     attn_grad = resid_grad.astype(jnp.bfloat16)
-    all_attn_grad = lax.all_gather(attn_grad, "ex", axis=0, tiled=True)
-    grad_w_attn_out = contract_rows(all_mixed, all_attn_grad)
     mixed_grad = (
         contract_cols(attn_grad, w_attn_out)
         .astype(jnp.bfloat16)
@@ -539,7 +676,8 @@
         + contract_cols(key_grad, w_key)
         + contract_cols(value_flat, w_value)
     )
-    input_grad = sum_over_tp(input_part, 4).astype(jnp.float32)
+    input_sum, quarter_grad = sum_over_tp(4, input_part, own_quarter(attn_grad))
+    input_grad = input_sum.astype(jnp.float32)
     grad_gain_attn = jnp.sum(input_grad * normed_a, 0)
     normed_grad_a = input_grad * gain_attn
     grad_inputs = (
@@ -562,8 +700,21 @@
     small_rows = jnp.pad(small_rows, ((0, -small_rows.shape[0] % 16), (0, 0)))
     wide = jnp.concatenate([query_grad, key_grad, value_flat], 1)
     wide = jnp.pad(wide, ((0, 0), (0, -wide.shape[1] % 128)))
-    all_wide, all_small = gather_blocks("ex", 5, wide, small_rows.astype(jnp.bfloat16))
-    projections = contract_rows(all_attn_in, all_wide.reshape(ex_devices * tok_rows, -1))
+    all_wide, all_small, all_attn_in, all_attn_grad = gather_blocks(
+        5,
+        (("ex", False), ("ex", False), ("tp", True), ("tp", True)),
+        wide,
+        small_rows.astype(jnp.bfloat16),
+        quarter_in,
+        quarter_grad,
+    )
+    every = ex_devices * tok_rows
+    projections = contract_rows(
+        all_attn_in.reshape(every, model_width), all_wide.reshape(every, -1)
+    )
+    grad_w_attn_out = contract_rows(
+        all_mixed.reshape(every, -1), all_attn_grad.reshape(every, model_width)
+    )
     small_sum = jnp.sum(all_small.astype(jnp.float32), 0)
     return (
         output,

time: 209 us -> 156 us (0.75)
  blocking collectives: 28.2 us -> 0 us
  between operations: 14.8 us -> 1.48 us
  Pallas kernels: 115 us -> 110 us
  matrix products: 26.4 us -> 22.8 us
    all_gather x1 -> x0, blocking collectives: 28.2 us -> none  [shards(): all_mixed = lax.all_gather(mixed_heads, 'ex', axis=0, tiled=True)]
    pallas_call x6, Pallas kernels: 115 us -> 110 us  [call_kernel(): pl.pallas_call(body, out_shape=out_shapes, in_specs=[pl.BlockSpec(memory_...]
    dot_general x5, matrix products: 11.8 us -> 8.8 us  [contract_rows(): lax.dot_general(left_side, right_side, (((0,), (0,)), ((), ())), preferre...]
    unnamed x82 -> x78, local copies, waits for them, and re-layouts: 4.5 us -> 4.52 us
  transfers between devices with their start and end apart: 2 -> 0, of which waited for: 0 -> 0; matrix products, arithmetic and copies ran while one was open for 19% -> 0% of each run, Pallas kernels for 55% -> 0%
where the time goes in v3:
time: 156 us
  Pallas kernels  110 us (71%)
  matrix products  22.8 us (15%)
  local copies, waits for them, and re-layouts  12.4 us (8%)
  other arithmetic  9.46 us (6%)
    pallas_call x6, Pallas kernels, call_kernel(): pl.pallas_call(body, out_shape=out_shapes, in_specs=[pl.BlockSpec(memory_...  110 us
    dot_general x5, matrix products, contract_rows(): lax.dot_general(left_side, right_side, (((0,), (0,)), ((), ())), preferre...  8.8 us
    unnamed x78, local copies, waits for them, and re-layouts  4.52 us
    dot_general x6, matrix products, contract_cols(): lax.dot_general(left_side, right_side, (((1,), (1,)), ((), ())), preferre...  3.38 us

profile of v3, /device:TPU:0, one launch (start us, length us, event | category | flops | bytes accessed | tf_op | source)
XLA Modules:
  0.0 155.8 jit_solution(12538323104667723707)
XLA Ops:
  0.7 1.2 fusion.37
  1.9 1.1 fusion.34
  2.9 1.2 convolution_convert_fusion.6
  4.3 1.4 fusion.1
  5.9 0.2 convolution_convert_fusion.7
  6.5 0.3 fusion.91
  6.8 0.2 convolution_convert_fusion.8
  7.6 21.3 %shard_map.229 = (bf16[128,768]{1,0:T(8,128)(2,1)S(1)}, bf16[8,32,768]{2,1,0:T(8,128)(2,1)S(1)}, bf16[8,128,192]{2,1,0:T(8,128)(2,1)S(1)}) custom-call(f32[128,768]{1,0:T(8,128)S(1)} %fusion.92.refs_0_, bf16[32,768]{1,0:T(8,128)(2,1)S(1)} %constant_dynamic-slice_fusion.1.refs_1_, bf16[128,192]{1,0:T(8,128)(2,1)S(1)} %copy.129.refs_2_), custom_call_target="tpu_custom_call" | custom-call | tf_op jit(solution)/shard_map/pallas_call | solution.py:367
  30.4 0.2 slice_reduce_fusion.1
  30.8 1.0 convolution_convert_fusion.2
  31.7 19.9 %shard_map.230 = bf16[4,8,64,384]{3,2,1,0:T(8,128)(2,1)S(1)} custom-call(bf16[8,64,384]{2,1,0:T(8,128)(2,1)S(1)} %bitcast.113), custom_call_target="tpu_custom_call" | custom-call | tf_op jit(solution)/shard_map/pallas_call | solution.py:367
  51.9 0.8 fusion.15
  53.1 0.8 copy-done.34
  53.8 1.5 fusion.8
  55.3 0.9 copy-done.17
  56.2 0.8 convolution_convert_fusion
  57.1 1.1 convolution_convert_fusion.1
  58.3 0.2 pad_maximum_fusion.x_ref
  58.5 19.9 %shard_map.231 = bf16[8,64,384]{2,1,0:T(8,128)(2,1)S(1)} custom-call(bf16[4,8,64,384]{3,2,1,0:T(8,128)(2,1)S(1)} %pad_maximum_fusion.x_ref), custom_call_target="tpu_custom_call" | custom-call | tf_op jit(solution)/shard_map/pallas_call | solution.py:367
  78.5 0.4 fusion.29
  78.8 0.8 convert_element_type.287
  79.6 1.7 %multiply_reduce_fusion.5 = (f32[128]{0:T(128)S(1)}, f32[128]{0:T(128)S(1)}, bf16[128,384]{1,0:T(8,128)(2,1)}) fusion(f32[256,384]{1,0:T(8,128)S(1)} %fusion.29, f32[128,768]{1,0:T(8,128)} %convert_element_type.287, s32[]{:T(128)S(6)} %select_n.56, f32[128]{0:T(128)S(1)} %get-tuple-element.143, f32[128]{0:T(128)S(1)} %get-tuple-element.144), kind=kLoop, calls=%fused_computation.102 | loop fusion | flops 392960 | bytes 690180 | tf_op jit(solution)/shard_map/reduce_sum | solution.py:600
  81.7 1.0 maximum_maximum_fusion.refs_0_
  82.7 6.1 %shard_map.232 = bf16[4,128,512]{2,1,0:T(8,128)(2,1)S(1)} custom-call(bf16[128,512]{1,0:T(8,128)(2,1)S(1)} %maximum_maximum_fusion.refs_0_), custom_call_target="tpu_custom_call" | custom-call | tf_op jit(solution)/shard_map/pallas_call | solution.py:367
  88.9 1.0 copy-done.2
  90.3 1.3 slice_bitcast_fusion.1
  91.6 1.0 multiply_reduce_fusion
  92.9 0.2 convolution_convert_fusion.5
  93.1 0.3 multiply_reduce_fusion.3
  93.6 0.4 fusion.94
  94.3 0.2 convolution_add_fusion.1
  94.7 0.6 copy-done.18
  95.3 0.2 convolution_add_fusion.refs_0_
  95.6 14.5 %shard_map.233 = (bf16[128,768]{1,0:T(8,128)(2,1)S(1)}, bf16[8,32,768]{2,1,0:T(8,128)(2,1)S(1)}) custom-call(f32[128,768]{1,0:T(8,128)S(1)} %convolution_add_fusion.refs_0_, bf16[32,768]{1,0:T(8,128)(2,1)S(1)} %constant_dynamic-slice_fusion.refs_1_), custom_call_target="tpu_custom_call" | custom-call | tf_op jit(solution)/shard_map/pallas_call | solution.py:367
  110.1 0.3 fusion.36
  110.4 1.0 fusion.33
  111.4 0.9 copy.143
  112.5 0.9 copy.141
  113.6 1.9 %fusion.22 = bf16[32,3]{0,1:T(4,128)(2,1)S(1)} fusion(f32[3,128,128]{2,0,1:T(4,128)S(1)} %copy.144, s32[128,128]{1,0:T(8,128)} %copy-done.26), kind=kOutput, calls=%fused_computation.43 | convolution fusion | flops 19398752 | bytes 262336 | tf_op jit(solution)/shard_map/hij,bij->bh/dot_general | solution.py:655
  116.1 27.9 %shard_map.234 = (bf16[8,128,640]{2,1,0:T(8,128)(2,1)S(1)}, bf16[8,16,768]{2,1,0:T(8,128)(2,1)S(1)}, bf16[8,4,32,768]{3,2,1,0:T(8,128)(2,1)S(1)}, bf16[8,4,32,768]{3,2,1,0:T(8,128)(2,1)S(1)}) custom-call(bf16[128,640]{1,0:T(8,128)(2,1)S(1)} %fusion.53.refs_0_, bf16[16,768]{1,0:T(8,128)(2,1)S(1)} %pad.16.refs_1_, ...), custom_call_target="tpu_custom_call" | custom-call | tf_op jit(solution)/shard_map/pallas_call | solution.py:367
  144.0 1.3 fusion.95
  145.3 1.2 fusion.87
  146.6 1.3 fusion.96
  147.9 0.6 slice_reduce_fusion.4
  148.6 0.7 copy.146
  149.3 0.6 slice_bitcast_fusion.4
  149.9 3.5 %convolution_bitcast_fusion.1 = f32[1,768,768]{2,1,0:T(8,128)} fusion(bf16[512,768]{1,0:T(8,128)(2,1)} %copy-done.17, bf16[512,384]{1,0:T(8,128)(2,1)S(1)} %bitcast.121, bf16[512,384]{1,0:T(8,128)(2,1)S(1)} %bitcast.123), kind=kOutput, calls=%fused_computation.6 | convolution fusion | flops 605552640 | bytes 3932160 | tf_op jit(solution)/shard_map/dot_general | solution.py:31
  153.4 2.4 %convolution_bitcast_fusion = f32[1,768,768]{2,1,0:T(8,128)} fusion(bf16[512,384]{1,0:T(8,128)(2,1)S(1)} %bitcast.143, bf16[512,384]{1,0:T(8,128)(2,1)S(1)} %bitcast.141, f32[512,768]{1,0:T(8,128)S(1)} %copy-done.37), kind=kOutput, calls=%fused_computation.5 | convolution fusion | flops 609091584 | bytes 4718592 | tf_op jit(solution)/shard_map/dot_general | solution.py:31
  (136 shorter events, 6.1 us)
Async XLA Ops:
  0.6 51.3 %copy-start = (bf16[1,768,768]{2,1,0:T(8,128)(2,1)S(1)}, bf16[1,768,768]{2,1,0:T(8,128)(2,1)}, u32[]{:S(2)}) copy-start(bf16[1,768,768]{2,1,0:T(8,128)(2,1)} %param.25) | copy-start | bytes 3538948
  0.7 5.2 %copy-start.12 = (bf16[768,192]{0,1:T(8,128)(2,1)S(1)}, bf16[768,192]{0,1:T(8,128)(2,1)}, u32[]{:S(2)}) copy-start(bf16[768,192]{0,1:T(8,128)(2,1)} %param.17) | copy-start | bytes 884740
  0.7 5.5 %copy-start.35 = (s32[1,4]{1,0:T(1,128)S(1)}, s32[1,4]{1,0:T(1,128)}, u32[]{:S(2)}) copy-start(s32[1,4]{1,0:T(1,128)} %param.16) | copy-start | bytes 52
  1.8 5.0 %copy-start.15 = (bf16[768,192]{0,1:T(8,128)(2,1)S(1)}, bf16[768,192]{0,1:T(8,128)(2,1)}, u32[]{:S(2)}) copy-start(bf16[768,192]{0,1:T(8,128)(2,1)} %param.19) | copy-start | bytes 884740
  4.2 3.1 %copy-start.10 = (bf16[192,768]{1,0:T(8,128)(2,1)S(1)}, bf16[192,768]{1,0:T(8,128)(2,1)}, u32[]{:S(2)}) copy-start(bf16[192,768]{1,0:T(8,128)(2,1)} %param.20) | copy-start | bytes 884740
  4.3 2.1 %copy-start.26 = (s32[128,128]{1,0:T(8,128)}, s32[128,128]{1,0:T(8,128)S(1)}, u32[]{:S(2)}) copy-start(s32[128,128]{1,0:T(8,128)S(1)} %compare_select_fusion) | copy-start | bytes 196612
  6.1 1.4 copy-start.20
  6.2 22.8 %copy-start.1 = (bf16[128,768]{1,0:T(8,128)(2,1)S(1)}, bf16[128,768]{1,0:T(8,128)(2,1)}, u32[]{:S(2)}) copy-start(bf16[128,768]{1,0:T(8,128)(2,1)} %param.14) | copy-start | bytes 589828
  6.7 22.4 %copy-start.28 = (f32[768]{0:T(1024)S(1)}, f32[768]{0:T(1024)}, u32[]{:S(2)}) copy-start(f32[768]{0:T(1024)} %param.22) | copy-start | bytes 9220
  6.8 22.4 %copy-start.30 = (bf16[768,8]{0,1:T(8,128)(2,1)S(1)}, bf16[768,8]{0,1:T(8,128)(2,1)}, u32[]{:S(2)}) copy-start(bf16[768,8]{0,1:T(8,128)(2,1)} %param.24) | copy-start | bytes 36868
  7.1 22.3 %copy-start.29 = (s32[128,2]{0,1:T(2,128)S(1)}, s32[128,2]{0,1:T(2,128)}, u32[]{:S(2)}) copy-start(s32[128,2]{0,1:T(2,128)} %param.15) | copy-start | bytes 3076
  7.3 23.4 %copy-start.3 = (bf16[128,768]{1,0:T(8,128)(2,1)S(1)}, bf16[128,768]{1,0:T(8,128)(2,1)}, u32[]{:S(2)}) copy-start(bf16[128,768]{1,0:T(8,128)(2,1)} %param.27) | copy-start | bytes 589828
  29.1 63.5 %copy-start.31 = (f32[128]{0:T(128)}, f32[128]{0:T(128)S(1)}, u32[]{:S(2)}) copy-start(f32[128]{0:T(128)S(1)} %add_rsqrt_fusion) | copy-start | bytes 1540
  29.2 22.5 %copy-start.4 = (bf16[128,768]{1,0:T(8,128)(2,1)}, bf16[128,768]{1,0:T(8,128)(2,1)S(1)}, u32[]{:S(2)}) copy-start(bf16[128,768]{1,0:T(8,128)(2,1)S(1)} %multiply_convert_fusion.3) | copy-start | bytes 589828
  51.9 0.9 copy-start.6
  51.9 0.9 copy-start.8
  51.9 1.0 copy-start.22
  51.9 1.1 copy-start.24
  51.9 1.9 %copy-start.34 = (bf16[1,768,768]{2,1,0:T(8,128)(2,1)S(1)}, bf16[1,768,768]{2,1,0:T(8,128)(2,1)}, u32[]{:S(2)}) copy-start(bf16[1,768,768]{2,1,0:T(8,128)(2,1)} %param.26) | copy-start | bytes 3538948
  52.8 4.3 %copy-start.36 = (f32[512,768]{1,0:T(8,128)}, f32[512,768]{1,0:T(8,128)S(1)}, u32[]{:S(2)}) copy-start(f32[512,768]{1,0:T(8,128)S(1)} %fusion.15) | copy-start | bytes 4718596
  55.3 0.9 copy-start.17
  88.9 1.0 copy-start.2
  91.6 1.3 copy-start.11
  92.6 1.0 copy-start.13
  92.9 1.2 copy-start.21
  92.9 1.4 copy-start.14
  93.4 1.9 %copy-start.16 = (bf16[768,192]{0,1:T(8,128)(2,1)S(1)}, bf16[768,192]{0,1:T(8,128)(2,1)}, u32[]{:S(2)}) copy-start(bf16[768,192]{0,1:T(8,128)(2,1)} %param.19) | copy-start | bytes 884740
  93.6 0.6 copy-start.19
  94.2 15.8 %copy-start.27 = (f32[768]{0:T(1024)S(1)}, f32[768]{0:T(1024)}, u32[]{:S(2)}) copy-start(f32[768]{0:T(1024)} %param.21) | copy-start | bytes 9220
  94.2 16.1 %copy-start.32 = (f32[128]{0:T(128)S(1)}, f32[128]{0:T(128)}, u32[]{:S(2)}) copy-start(f32[128]{0:T(128)} %copy-done.31) | copy-start | bytes 1540
  94.7 0.6 copy-start.18
  110.4 5.6 %copy-start.33 = (bf16[768]{0:T(1024)(128)(2,1)S(1)}, bf16[768]{0:T(1024)(128)(2,1)}, u32[]{:S(2)}) copy-start(bf16[768]{0:T(1024)(128)(2,1)} %get-tuple-element.102) | copy-start | bytes 4612
  111.4 4.4 %copy-start.5 = (bf16[128,768]{1,0:T(8,128)(2,1)S(1)}, bf16[128,768]{1,0:T(8,128)(2,1)}, u32[]{:S(2)}) copy-start(bf16[128,768]{1,0:T(8,128)(2,1)} %copy-done.4) | copy-start | bytes 589828
  146.5 3.4 %copy-start.7 = (bf16[1,8,64,384]{3,2,1,0:T(8,128)(2,1)S(1)}, bf16[1,8,64,384]{3,2,1,0:T(8,128)(2,1)}, u32[]{:S(2)}) copy-start(bf16[1,8,64,384]{3,2,1,0:T(8,128)(2,1)} %copy-done.6) | copy-start | bytes 1179652
  146.6 3.4 %copy-start.9 = (bf16[1,8,64,384]{3,2,1,0:T(8,128)(2,1)S(1)}, bf16[1,8,64,384]{3,2,1,0:T(8,128)(2,1)}, u32[]{:S(2)}) copy-start(bf16[1,8,64,384]{3,2,1,0:T(8,128)(2,1)} %copy-done.8) | copy-start | bytes 1179652
  149.9 3.5 %copy-start.23 = (bf16[1,8,64,384]{3,2,1,0:T(8,128)(2,1)S(1)}, bf16[1,8,64,384]{3,2,1,0:T(8,128)(2,1)}, u32[]{:S(2)}) copy-start(bf16[1,8,64,384]{3,2,1,0:T(8,128)(2,1)} %copy-done.22) | copy-start | bytes 1179652
  149.9 3.5 %copy-start.25 = (bf16[1,8,64,384]{3,2,1,0:T(8,128)(2,1)S(1)}, bf16[1,8,64,384]{3,2,1,0:T(8,128)(2,1)}, u32[]{:S(2)}) copy-start(bf16[1,8,64,384]{3,2,1,0:T(8,128)(2,1)} %copy-done.24) | copy-start | bytes 1179652
  149.9 3.5 %copy-start.37 = (f32[512,768]{1,0:T(8,128)S(1)}, f32[512,768]{1,0:T(8,128)}, u32[]{:S(2)}) copy-start(f32[512,768]{1,0:T(8,128)} %copy-done.36) | copy-start | bytes 4718596

commit v4 on v3

--- a/solution.py
+++ b/solution.py
@@ -503,9 +503,16 @@
     def own_quarter(rows):
         return lax.dynamic_slice_in_dim(rows, tp_index * quarter, quarter, 0)
 
-    head_sum, quarter_in, all_mixed = sum_over_tp(
-        0, head_part, own_quarter(attn_in), mixed_heads
-    )
+    mixed_width = mixed_heads.shape[1]
+    early_rows = lax.all_gather(
+        jnp.concatenate(
+            [attn_in, jnp.pad(mixed_heads, ((0, 0), (0, -mixed_width % 128)))], 1
+        ),
+        "ex",
+        axis=0,
+        tiled=True,
+    )
+    [head_sum] = sum_over_tp(0, head_part)
     residual = inputs_f + head_sum.astype(jnp.float32)
     scale_m = rms_scale(residual)
     normed_m = residual * scale_m
@@ -700,20 +707,19 @@
     small_rows = jnp.pad(small_rows, ((0, -small_rows.shape[0] % 16), (0, 0)))
     wide = jnp.concatenate([query_grad, key_grad, value_flat], 1)
     wide = jnp.pad(wide, ((0, 0), (0, -wide.shape[1] % 128)))
-    all_wide, all_small, all_attn_in, all_attn_grad = gather_blocks(
+    all_wide, all_small, all_attn_grad = gather_blocks(
         5,
-        (("ex", False), ("ex", False), ("tp", True), ("tp", True)),
+        (("ex", False), ("ex", False), ("tp", True)),
         wide,
         small_rows.astype(jnp.bfloat16),
-        quarter_in,
         quarter_grad,
     )
     every = ex_devices * tok_rows
     projections = contract_rows(
-        all_attn_in.reshape(every, model_width), all_wide.reshape(every, -1)
+        early_rows[:, :model_width], all_wide.reshape(every, -1)
     )
     grad_w_attn_out = contract_rows(
-        all_mixed.reshape(every, -1), all_attn_grad.reshape(every, model_width)
+        early_rows[:, model_width : model_width + mixed_width], all_attn_grad.reshape(every, model_width)
     )
     small_sum = jnp.sum(all_small.astype(jnp.float32), 0)
     return (

time: 156 us -> 169 us (1.083)
  between operations: 1.48 us -> 15 us
  Pallas kernels: 110 us -> 101 us
  matrix products: 22.8 us -> 28.4 us
  local copies, waits for them, and re-layouts: 12.4 us -> 15.1 us
    pallas_call x6, Pallas kernels: 110 us -> 101 us  [call_kernel(): pl.pallas_call(body, out_shape=out_shapes, in_specs=[pl.BlockSpec(memory_...]
    dot_general x5, matrix products: 8.8 us -> 11.8 us  [contract_rows(): lax.dot_general(left_side, right_side, (((0,), (0,)), ((), ())), preferre...]
    dot_general x6, matrix products: 3.38 us -> 5.25 us  [contract_cols(): lax.dot_general(left_side, right_side, (((1,), (1,)), ((), ())), preferre...]
    unnamed x78 -> x96, local copies, waits for them, and re-layouts: 4.52 us -> 4.43 us
  transfers between devices with their start and end apart: 0 -> 1, of which waited for: 0 -> 0; matrix products, arithmetic and copies ran while one was open for 0% -> 21% of each run, Pallas kernels for 0% -> 60%
where the time goes in v4:
time: 169 us; the launch traced here: 168 us
  Pallas kernels  101 us (60%)
  matrix products  28.4 us (17%)
  local copies, waits for them, and re-layouts  15.1 us (9%)
  between operations  15 us (9%)
  other arithmetic  8.88 us (5%)
    pallas_call x6, Pallas kernels, call_kernel(): pl.pallas_call(body, out_shape=out_shapes, in_specs=[pl.BlockSpec(memory_...  101 us
    dot_general x5, matrix products, contract_rows(): lax.dot_general(left_side, right_side, (((0,), (0,)), ((), ())), preferre...  11.8 us
    dot_general x6, matrix products, contract_cols(): lax.dot_general(left_side, right_side, (((1,), (1,)), ((), ())), preferre...  5.25 us
    unnamed x96, local copies, waits for them, and re-layouts  4.43 us
  transfers between devices with their start and end apart: 1, of which 0 were waited for; matrix products, arithmetic and copies ran while one was open for 21% of the time, Pallas kernels for 60%

profile of v4, /device:TPU:0, one launch (start us, length us, event | category | flops | bytes accessed | tf_op | source)
XLA Modules:
  0.0 168.0 jit_solution(16894318562781785595)
XLA Ops:
  7.4 1.2 fusion.42
  8.6 1.5 fusion.1
  10.2 1.0 fusion.39
  11.5 0.2 convolution_convert_fusion.7
  12.1 0.3 fusion.97
  12.4 0.2 convolution_convert_fusion.8
  13.0 0.7 fusion.48
  14.1 11.5 %shard_map.229 = bf16[128,768]{1,0:T(8,128)(2,1)S(1)} custom-call(f32[128,768]{1,0:T(8,128)S(1)} %fusion.98.refs_0_), custom_call_target="tpu_custom_call" | custom-call | tf_op jit(solution)/shard_map/pallas_call | solution.py:367
  25.9 0.5 copy-done.38
  27.4 0.8 convert_element_type.289
  28.6 1.0 convolution_convert_fusion.2
  29.6 23.5 %shard_map.230 = bf16[4,8,64,384]{3,2,1,0:T(8,128)(2,1)S(1)} custom-call(bf16[8,64,384]{2,1,0:T(8,128)(2,1)S(1)} %bitcast.108), custom_call_target="tpu_custom_call" | custom-call | tf_op jit(solution)/shard_map/pallas_call | solution.py:367
  53.4 1.3 copy-done.43
  54.7 0.8 fusion.17
  55.5 1.1 convolution_convert_fusion.1
  56.6 2.4 %fusion.8 = bf16[512,768]{1,0:T(8,128)(2,1)} fusion(f32[512,768]{1,0:T(8,128)S(1)} %fusion.17, bf16[1,768,768]{2,1,0:T(8,128)(2,1)S(1)} %copy-done, bf16[512,384]{1,0:T(8,128)(2,1)S(1)} %bitcast.136, bf16[512,384]{1,0:T(8,128)(2,1)S(1)} %bitcast.134), kind=kOutput, calls=%fused_computation.13 | convolution fusion | flops 613416960 | bytes 4325376 | tf_op jit(solution)/shard_map/dot_general | solution.py:37
  59.0 1.9 %convolution_convert_fusion = bf16[512,768]{1,0:T(8,128)(2,1)S(1)} fusion(bf16[512,768]{1,0:T(8,128)(2,1)} %fusion.8, bf16[1,768,768]{2,1,0:T(8,128)(2,1)S(1)} %copy-done.43), kind=kOutput, calls=%fused_computation.18 | convolution fusion | flops 604372992 | bytes 2752512 | tf_op jit(solution)/shard_map/dot_general | solution.py:37
  61.1 0.2 pad_maximum_fusion.x_ref
  61.4 20.7 %shard_map.231 = bf16[8,64,384]{2,1,0:T(8,128)(2,1)S(1)} custom-call(bf16[4,8,64,384]{3,2,1,0:T(8,128)(2,1)S(1)} %pad_maximum_fusion.x_ref), custom_call_target="tpu_custom_call" | custom-call | tf_op jit(solution)/shard_map/pallas_call | solution.py:367
  82.0 0.4 fusion.33
  83.1 6.2 %shard_map.232 = bf16[4,128,512]{2,1,0:T(8,128)(2,1)S(1)} custom-call(bf16[128,512]{1,0:T(8,128)(2,1)S(1)} %maximum_maximum_fusion.refs_0_), custom_call_target="tpu_custom_call" | custom-call | tf_op jit(solution)/shard_map/pallas_call | solution.py:367
  89.5 0.9 slice_bitcast_fusion.1
  90.7 1.5 multiply_reduce_fusion
  92.5 0.2 convolution_convert_fusion.5
  92.8 0.3 multiply_reduce_fusion.3
  93.2 0.8 copy.143
  94.1 0.8 copy.144
  94.9 0.3 fusion.22
  95.2 0.7 copy.142
  96.0 0.9 fusion.21
  97.1 2.1 %fusion.24 = bf16[32,3]{0,1:T(4,128)(2,1)S(1)} fusion(f32[3,128,128]{2,0,1:T(4,128)} %copy.144, s32[128,128]{1,0:T(8,128)} %copy-done.29), kind=kOutput, calls=%fused_computation.45 | convolution fusion | flops 19398752 | bytes 262336 | tf_op jit(solution)/shard_map/hij,bij->bh/dot_general | solution.py:662
  100.2 14.2 %shard_map.233 = (bf16[128,768]{1,0:T(8,128)(2,1)S(1)}, bf16[8,32,768]{2,1,0:T(8,128)(2,1)S(1)}) custom-call(f32[128,768]{1,0:T(8,128)S(1)} %convolution_add_fusion.refs_0_, bf16[32,768]{1,0:T(8,128)(2,1)S(1)} %constant_dynamic-slice_fusion.refs_1_), custom_call_target="tpu_custom_call" | custom-call | tf_op jit(solution)/shard_map/pallas_call | solution.py:367
  114.4 0.8 fusion.41
  115.6 24.5 %shard_map.234 = (bf16[8,128,640]{2,1,0:T(8,128)(2,1)S(1)}, bf16[8,16,768]{2,1,0:T(8,128)(2,1)S(1)}, bf16[8,4,32,768]{3,2,1,0:T(8,128)(2,1)S(1)}) custom-call(bf16[128,640]{1,0:T(8,128)(2,1)S(1)} %fusion.59.refs_0_, bf16[16,768]{1,0:T(8,128)(2,1)S(1)} %pad.21.refs_1_, bf16[8,32,768]{2,1,0:T(8,128)(2,1)S(1)} %get-tuple-element.18.refs_2_), custom_call_target="tpu_custom_call" | custom-call | tf_op jit(solution)/shard_map/pallas_call | solution.py:367
  140.1 1.0 copy-done.1
  141.2 0.6 copy-done.28
  141.8 0.5 slice_reduce_fusion.6
  142.3 0.7 reshape_squeeze.3
  143.1 0.7 copy.146
  143.7 1.4 slice_reduce_fusion.4
  145.2 0.7 broadcast_multiply_fusion
  145.8 1.4 slice_bitcast_fusion.4
  147.3 3.7 %convolution_bitcast_fusion.1 = f32[1,768,768]{2,1,0:T(8,128)} fusion(bf16[512,768]{1,0:T(8,128)(2,1)} %fusion.8, bf16[512,384]{1,0:T(8,128)(2,1)} %bitcast.115, bf16[512,384]{1,0:T(8,128)(2,1)} %bitcast.117), kind=kOutput, calls=%fused_computation.6 | convolution fusion | flops 605552640 | bytes 3932160 | tf_op jit(solution)/shard_map/dot_general | solution.py:31
  151.1 1.0 fusion.38
  152.2 2.4 %convolution_bitcast_fusion = f32[1,768,768]{2,1,0:T(8,128)} fusion(bf16[512,384]{1,0:T(8,128)(2,1)S(1)} %bitcast.137, bf16[512,384]{1,0:T(8,128)(2,1)S(1)} %bitcast.135, f32[512,768]{1,0:T(8,128)S(1)} %copy-done.46), kind=kOutput, calls=%fused_computation.5 | convolution fusion | flops 609091584 | bytes 4718592 | tf_op jit(solution)/shard_map/dot_general | solution.py:31
  154.5 3.0 %fusion.9 = f32[768,640]{0,1:T(8,128)S(1)} fusion(bf16[1024,640]{1,0:T(8,128)(2,1)} %bitcast.109, bf16[1024,1024]{1,0:T(8,128)(2,1)} %all-gather.2.cloned.1.call-done), kind=kOutput, calls=%fused_computation.14 | convolution fusion | flops 1006632960 | bytes 4849664 | tf_op jit(solution)/shard_map/dot_general | solution.py:31
  157.6 1.2 fusion.93
  158.8 2.4 %fusion.31 = f32[192,768]{1,0:T(8,128)} fusion(bf16[1024,768]{1,0:T(8,128)(2,1)S(1)} %bitcast.106, bf16[1024,1024]{1,0:T(8,128)(2,1)} %all-gather.2.cloned.1.call-done), kind=kOutput, calls=%fused_computation.61 | convolution fusion | flops 301989888 | bytes 2686976 | tf_op jit(solution)/shard_map/dot_general | solution.py:31
  (157 shorter events, 6.7 us)
Async XLA Ops:
  7.2 48.3 %copy-start = (bf16[1,768,768]{2,1,0:T(8,128)(2,1)S(1)}, bf16[1,768,768]{2,1,0:T(8,128)(2,1)}, u32[]{:S(2)}) copy-start(bf16[1,768,768]{2,1,0:T(8,128)(2,1)} %param.26) | copy-start | bytes 3538948
  7.2 4.1 %copy-start.12 = (bf16[768,192]{0,1:T(8,128)(2,1)S(1)}, bf16[768,192]{0,1:T(8,128)(2,1)}, u32[]{:S(2)}) copy-start(bf16[768,192]{0,1:T(8,128)(2,1)} %param.18) | copy-start | bytes 884740
  7.2 4.3 %copy-start.10 = (bf16[768,192]{0,1:T(8,128)(2,1)S(1)}, bf16[768,192]{0,1:T(8,128)(2,1)}, u32[]{:S(2)}) copy-start(bf16[768,192]{0,1:T(8,128)(2,1)} %param.17) | copy-start | bytes 884740
  7.2 4.6 %copy-start.44 = (s32[1,4]{1,0:T(1,128)S(1)}, s32[1,4]{1,0:T(1,128)}, u32[]{:S(2)}) copy-start(s32[1,4]{1,0:T(1,128)} %param.16) | copy-start | bytes 52
  7.2 147.3 %all-gather.2.cloned.1.call-start = ((), (), s32[]{:S(2)}) async-start(), calls=%async_computation | async-start | bytes 2359296 | tf_op jit(solution)/shard_map/all_gather | solution.py:507
  7.4 2.7 %copy-start.29 = (s32[128,128]{1,0:T(8,128)}, s32[128,128]{1,0:T(8,128)S(1)}, u32[]{:S(2)}) copy-start(s32[128,128]{1,0:T(8,128)S(1)} %compare_select_fusion) | copy-start | bytes 196612
  8.6 105.8 %copy-start.36 = (f32[128]{0:T(128)}, f32[128]{0:T(128)S(1)}, u32[]{:S(2)}) copy-start(f32[128]{0:T(128)S(1)} %add_rsqrt_fusion.1) | copy-start | bytes 1540
  8.6 3.9 %copy-start.14 = (bf16[768,192]{0,1:T(8,128)(2,1)S(1)}, bf16[768,192]{0,1:T(8,128)(2,1)}, u32[]{:S(2)}) copy-start(bf16[768,192]{0,1:T(8,128)(2,1)} %param.19) | copy-start | bytes 884740
  11.5 1.2 copy-start.19
  11.5 2.3 %copy-start.8 = (bf16[192,768]{1,0:T(8,128)(2,1)S(1)}, bf16[192,768]{1,0:T(8,128)(2,1)}, u32[]{:S(2)}) copy-start(bf16[192,768]{1,0:T(8,128)(2,1)} %param.20) | copy-start | bytes 884740
  11.8 0.9 copy-start.20
  12.4 13.2 %copy-start.2 = (bf16[128,768]{1,0:T(8,128)(2,1)S(1)}, bf16[128,768]{1,0:T(8,128)(2,1)}, u32[]{:S(2)}) copy-start(bf16[128,768]{1,0:T(8,128)(2,1)} %param.14) | copy-start | bytes 589828
  12.7 13.0 %copy-start.34 = (s32[128,2]{0,1:T(2,128)S(1)}, s32[128,2]{0,1:T(2,128)}, u32[]{:S(2)}) copy-start(s32[128,2]{0,1:T(2,128)} %param.15) | copy-start | bytes 3076
  12.7 13.6 %copy-start.32 = (f32[768]{0:T(1024)S(1)}, f32[768]{0:T(1024)}, u32[]{:S(2)}) copy-start(f32[768]{0:T(1024)} %param.22) | copy-start | bytes 9220
  13.0 13.4 %copy-start.35 = (bf16[768,8]{0,1:T(8,128)(2,1)S(1)}, bf16[768,8]{0,1:T(8,128)(2,1)}, u32[]{:S(2)}) copy-start(bf16[768,8]{0,1:T(8,128)(2,1)} %param.24) | copy-start | bytes 36868
  13.8 13.6 %copy-start.3 = (bf16[128,768]{1,0:T(8,128)(2,1)S(1)}, bf16[128,768]{1,0:T(8,128)(2,1)}, u32[]{:S(2)}) copy-start(bf16[128,768]{1,0:T(8,128)(2,1)} %param.27) | copy-start | bytes 589828
  25.7 0.6 copy-start.38
  53.1 1.6 copy-start.43
  53.3 3.2 %copy-start.6 = (bf16[1,8,64,384]{3,2,1,0:T(8,128)(2,1)}, bf16[1,8,64,384]{3,2,1,0:T(8,128)(2,1)S(1)}, u32[]{:S(2)}) copy-start(bf16[1,8,64,384]{3,2,1,0:T(8,128)(2,1)S(1)} %get-tuple-element.115) | copy-start | bytes 1179652
  53.3 3.2 %copy-start.7 = (bf16[1,8,64,384]{3,2,1,0:T(8,128)(2,1)}, bf16[1,8,64,384]{3,2,1,0:T(8,128)(2,1)S(1)}, u32[]{:S(2)}) copy-start(bf16[1,8,64,384]{3,2,1,0:T(8,128)(2,1)S(1)} %get-tuple-element.116) | copy-start | bytes 1179652
  53.3 3.2 %copy-start.22 = (bf16[1,8,64,384]{3,2,1,0:T(8,128)(2,1)}, bf16[1,8,64,384]{3,2,1,0:T(8,128)(2,1)S(1)}, u32[]{:S(2)}) copy-start(bf16[1,8,64,384]{3,2,1,0:T(8,128)(2,1)S(1)} %get-tuple-element.113) | copy-start | bytes 1179652
  53.4 3.2 %copy-start.24 = (bf16[1,8,64,384]{3,2,1,0:T(8,128)(2,1)}, bf16[1,8,64,384]{3,2,1,0:T(8,128)(2,1)S(1)}, u32[]{:S(2)}) copy-start(bf16[1,8,64,384]{3,2,1,0:T(8,128)(2,1)S(1)} %get-tuple-element.114) | copy-start | bytes 1179652
  55.4 1.1 copy-start.45
  61.4 21.1 %copy-start.16 = (f32[128,768]{1,0:T(8,128)S(1)}, f32[128,768]{1,0:T(8,128)}, u32[]{:S(2)}) copy-start(f32[128,768]{1,0:T(8,128)} %convert_element_type.289) | copy-start | bytes 1179652
  89.4 1.3 copy-start.39
  90.4 2.1 %copy-start.9 = (bf16[192,768]{1,0:T(8,128)(2,1)S(1)}, bf16[192,768]{1,0:T(8,128)(2,1)}, u32[]{:S(2)}) copy-start(bf16[192,768]{1,0:T(8,128)(2,1)} %param.20) | copy-start | bytes 884740
  92.3 1.7 %copy-start.4 = (f32[128,768]{1,0:T(8,128)}, f32[128,768]{1,0:T(8,128)S(1)}, u32[]{:S(2)}) copy-start(f32[128,768]{1,0:T(8,128)S(1)} %get-tuple-element.132) | copy-start | bytes 1179652
  92.3 1.8 %copy-start.41 = (f32[128]{0:T(128)}, f32[128]{0:T(128)S(1)}, u32[]{:S(2)}) copy-start(f32[128]{0:T(128)S(1)} %broadcast_multiply_fusion.1) | copy-start | bytes 1540
  92.3 2.6 %copy-start.21 = (bf16[128,192]{0,1:T(8,128)(2,1)S(1)}, bf16[128,192]{0,1:T(8,128)(2,1)}, u32[]{:S(2)}) copy-start(bf16[128,192]{0,1:T(8,128)(2,1)} %copy-done.20) | copy-start | bytes 147460
  93.0 6.4 %copy-start.11 = (bf16[768,192]{0,1:T(8,128)(2,1)S(1)}, bf16[768,192]{0,1:T(8,128)(2,1)}, u32[]{:S(2)}) copy-start(bf16[768,192]{0,1:T(8,128)(2,1)} %param.17) | copy-start | bytes 884740
  94.0 5.7 %copy-start.13 = (bf16[768,192]{0,1:T(8,128)(2,1)S(1)}, bf16[768,192]{0,1:T(8,128)(2,1)}, u32[]{:S(2)}) copy-start(bf16[768,192]{0,1:T(8,128)(2,1)} %param.18) | copy-start | bytes 884740
  95.2 4.7 %copy-start.15 = (bf16[768,192]{0,1:T(8,128)(2,1)S(1)}, bf16[768,192]{0,1:T(8,128)(2,1)}, u32[]{:S(2)}) copy-start(bf16[768,192]{0,1:T(8,128)(2,1)} %param.19) | copy-start | bytes 884740
  99.4 15.0 %copy-start.30 = (f32[768]{0:T(1024)S(1)}, f32[768]{0:T(1024)}, u32[]{:S(2)}) copy-start(f32[768]{0:T(1024)} %param.21) | copy-start | bytes 9220
  99.7 15.8 %copy-start.26 = (bf16[128,192]{1,0:T(8,128)(2,1)S(1)}, bf16[128,192]{1,0:T(8,128)(2,1)}, u32[]{:S(2)}) copy-start(bf16[128,192]{1,0:T(8,128)(2,1)} %copy.143) | copy-start | bytes 147460
  99.7 15.8 %copy-start.27 = (bf16[128,192]{1,0:T(8,128)(2,1)S(1)}, bf16[128,192]{1,0:T(8,128)(2,1)}, u32[]{:S(2)}) copy-start(bf16[128,192]{1,0:T(8,128)(2,1)} %copy.142) | copy-start | bytes 147460
  140.1 1.1 copy-start.1
  141.2 0.6 copy-start.28
  147.2 3.8 %copy-start.5 = (f32[128,768]{1,0:T(8,128)S(1)}, f32[128,768]{1,0:T(8,128)}, u32[]{:S(2)}) copy-start(f32[128,768]{1,0:T(8,128)} %copy-done.4) | copy-start | bytes 1179652
  147.2 3.8 %copy-start.17 = (f32[128,384]{1,0:T(8,128)S(1)}, f32[128,384]{1,0:T(8,128)}, u32[]{:S(2)}) copy-start(f32[128,384]{1,0:T(8,128)} %get-tuple-element.119) | copy-start | bytes 589828
  147.2 3.8 %copy-start.18 = (f32[128,384]{1,0:T(8,128)S(1)}, f32[128,384]{1,0:T(8,128)}, u32[]{:S(2)}) copy-start(f32[128,384]{1,0:T(8,128)} %get-tuple-element.120) | copy-start | bytes 589828
  147.2 3.8 %copy-start.31 = (f32[768]{0:T(1024)S(1)}, f32[768]{0:T(1024)}, u32[]{:S(2)}) copy-start(f32[768]{0:T(1024)} %param.21) | copy-start | bytes 9220
  147.2 3.8 %copy-start.33 = (f32[768]{0:T(1024)S(1)}, f32[768]{0:T(1024)}, u32[]{:S(2)}) copy-start(f32[768]{0:T(1024)} %param.22) | copy-start | bytes 9220
  147.3 3.8 %copy-start.37 = (f32[128]{0:T(128)S(1)}, f32[128]{0:T(128)}, u32[]{:S(2)}) copy-start(f32[128]{0:T(128)} %copy-done.36) | copy-start | bytes 1540
  147.3 3.8 %copy-start.40 = (f32[128]{0:T(128)S(1)}, f32[128]{0:T(128)}, u32[]{:S(2)}) copy-start(f32[128]{0:T(128)} %copy-done.38) | copy-start | bytes 1540
  147.3 3.8 %copy-start.42 = (f32[128]{0:T(128)S(1)}, f32[128]{0:T(128)}, u32[]{:S(2)}) copy-start(f32[128]{0:T(128)} %copy-done.41) | copy-start | bytes 1540
  147.3 4.9 %copy-start.46 = (f32[512,768]{1,0:T(8,128)S(1)}, f32[512,768]{1,0:T(8,128)}, u32[]{:S(2)}) copy-start(f32[512,768]{1,0:T(8,128)} %copy-done.45) | copy-start | bytes 4718596
  151.0 1.1 copy-start.23
  151.0 1.1 copy-start.25
Sparse Core Ops, SparseCore 0:
  13.9 57.7 all-gather.1
